TPU v7x, 128 devices: a whole 4x4x4 slice. The times are simulated.
128 devices in a mesh: tile: 32 (over x, y_hi, z), mode: 4 (over y_lo, core).
Axes of the slice: x: 4, y: 4 (y_hi: 2, y_lo: 2; y = y_hi * 2 + y_lo), z: 4, core: 2. Of those that a mesh axis runs over, the one named last changes fastest.
Arguments:
- object_real: float32 [32, 2, 384, 384], P('tile', None, 'mode'), may hold values from 0.6 to 1.2
- object_imag: float32 [32, 2, 384, 384], P('tile', None, 'mode'), may hold values from -0.4 to 0.4
- probe: float32 [2, 8, 256, 256], P(None, 'mode'), may hold values from -1.5 to 1.5
- measured: float32 [32, 2, 256, 256], P('tile'), may hold values from 0.2 to 1.6
- positions: int32 [32, 2, 2], P('tile'), may hold values from 0 to 128
Outputs:
- object_grad_real: float32 [32, 2, 384, 384], P('tile', None, 'mode')
- object_grad_imag: float32 [32, 2, 384, 384], P('tile', None, 'mode')
- probe_grad: float32 [2, 8, 256, 256], P(None, 'mode')
All inputs are finite; a program needn't handle non-finite values.
Results may differ from a plain program's by a relative error of at most 0.0003.
Values sent between devices are 32-bit elements; how exact they have to be, the bound alone decides.
A program may use at most 128 MiB of HBM per device.

v0:
```python
import functools
import math

import jax
import jax.numpy as jnp
import ml_dtypes
import numpy as np
from jax import lax
from jax.experimental import pallas as pl
from jax.experimental.pallas import tpu as pltpu
from jax.sharding import PartitionSpec as P

PX = 256
HALF = PX // 2
TILE = 384
MARGIN = 64
ROWS = 96
EDGE = TILE - PX
FLOOR = 0.1
FRESNEL = 40.0
MESH = pl.DeviceIdType.MESH
F32 = jnp.float32
BF16 = jnp.bfloat16

A_LEFT, A_RIGHT, F_LEFT, F_RIGHT, B_LEFT, B_RIGHT = range(6)


def real_form(c):
    return np.block([[c.real, -c.imag], [c.imag, c.real]])


@functools.cache
def constants():
    index = np.arange(PX)
    fourier = np.exp(-2j * np.pi * (np.outer(index, index) % PX) / PX) / math.sqrt(PX)
    freq = ((index + HALF) % PX - HALF) / PX
    chirp = np.exp(-1j * np.pi * FRESNEL * freq**2)
    through = fourier.conj() @ (chirp[:, None] * fourier)
    near, far = through[:HALF, :HALF], through[:HALF, HALF:]
    pairs = [None] * 6
    moved = [(near + far) / 2, (near - far) / 2]
    split = [fourier[0::2, :HALF], fourier[1::2, :HALF]]
    pairs[A_LEFT] = [real_form(c) for c in moved]
    pairs[A_RIGHT] = [real_form(c).T for c in moved]
    pairs[F_LEFT] = [real_form(c) for c in split]
    pairs[F_RIGHT] = [real_form(c).T for c in split]
    pairs[B_LEFT] = [real_form(c.T) for c in split]
    pairs[B_RIGHT] = [real_form(c.T).T for c in split]
    table = np.array(pairs).reshape(12, PX, PX)
    high = table.astype(ml_dtypes.bfloat16)
    low = (table - high.astype(np.float64)).astype(ml_dtypes.bfloat16)
    order = np.zeros((PX, PX))
    order[np.arange(HALF), np.arange(0, PX, 2)] = 1
    order[np.arange(HALF) + HALF, np.arange(1, PX, 2)] = 1
    orders = np.array([order, order.T]).astype(ml_dtypes.bfloat16)
    return np.stack([high, low], axis=1), orders


def two_parts(x):
    high = x.astype(BF16)
    return high, (x - high.astype(F32)).astype(BF16)


def product(a, b):
    return jnp.dot(a, b, preferred_element_type=F32)


def apply_left(table, kind, sign, z):
    high, low = two_parts(z)
    c_high, c_low = table[2 * kind + sign, 0], table[2 * kind + sign, 1]
    return product(
        jnp.concatenate([c_high, c_low, c_high], axis=1),
        jnp.concatenate([high, high, low], axis=0),
    )


def apply_right(table, kind, sign, z):
    high, low = two_parts(z)
    c_high, c_low = table[2 * kind + sign, 0], table[2 * kind + sign, 1]
    return product(
        jnp.concatenate([high, high, low], axis=1),
        jnp.concatenate([c_high, c_low, c_high], axis=0),
    )


def rows_first(x):
    return x[:HALF], x[HALF:]


def lanes_first(x):
    return x[:, :HALF], x[:, HALF:]


def one_side(table, kind, re, im, left):
    halves, axis, apply = (rows_first, 0, apply_left) if left else (lanes_first, 1, apply_right)
    (r0, r1), (i0, i1) = halves(re), halves(im)
    if kind[0] != B_LEFT:
        r0, r1, i0, i1 = r0 + r1, r0 - r1, i0 + i1, i0 - i1
    which = kind[0] if left else kind[1]
    plus = apply(table, which, 0, jnp.concatenate([r0, i0], axis=axis))
    minus = apply(table, which, 1, jnp.concatenate([r1, i1], axis=axis))
    (pr, pi), (mr, mi) = halves(plus), halves(minus)
    if kind[0] != F_LEFT:
        pr, mr, pi, mi = pr + mr, pr - mr, pi + mi, pi - mi
    return jnp.concatenate([pr, mr], axis=axis), jnp.concatenate([pi, mi], axis=axis)


def both_sides(table, kind, re, im):
    re, im = one_side(table, kind, re, im, True)
    return one_side(table, kind, re, im, False)


THROUGH = (A_LEFT, A_RIGHT)
FORTH = (F_LEFT, F_RIGHT)
BACK = (B_LEFT, B_RIGHT)


def times(ar, ai, br, bi):
    return ar * br - ai * bi, ar * bi + ai * br


def kernel(
    tiles,
    obj_re,
    obj_im,
    probe_in,
    measured_in,
    positions,
    table_in,
    orders_in,
    out_re,
    out_im,
    out_probe,
    tile0,
    tile1,
    crops,
    probe,
    measured,
    table,
    orders,
    wave1,
    far,
    ipart,
    isib,
    isum,
    icross,
    factor,
    crop_grad,
    rs_send,
    rs_got,
    rs_cross,
    rs_cross_got,
    own,
    edge_send,
    edge_got,
    local_sem,
    tile_local,
    g_send,
    g_recv,
    i_send,
    i_recv,
    r_send,
    r_recv,
    e_send,
    e_recv,
):
    t = lax.axis_index("tile")
    m = lax.axis_index("mode")
    core = lax.rem(m, 2)
    high = m // 2
    sibling = high * 2 + (1 - core)
    across = (1 - high) * 2 + core
    diagonal = (1 - high) * 2 + (1 - core)
    left = lax.rem(t + tiles - 1, tiles)
    right = lax.rem(t + 1, tiles)
    to_sibling, to_across = (t, sibling), (t, across)
    to_left, to_right = (left, m), (right, m)

    barrier = pltpu.get_barrier_semaphore()
    for device in (to_sibling, to_across, to_left, to_right):
        pl.semaphore_signal(barrier, inc=1, device_id=device, device_id_type=MESH)

    loads = [
        pltpu.make_async_copy(probe_in, probe, local_sem.at[0]),
        pltpu.make_async_copy(measured_in.at[0], measured, local_sem.at[1]),
        pltpu.make_async_copy(table_in, table, local_sem.at[2]),
        pltpu.make_async_copy(orders_in, orders, local_sem.at[3]),
    ]
    for load in loads:
        load.start()

    whole = (tile0, tile1)
    objects = (obj_re, obj_im)

    def my_rows(who):
        return pl.ds(pl.multiple_of(who * ROWS, ROWS), ROWS)

    def remote(src, dst, send, recv, device):
        return pltpu.make_async_remote_copy(
            src_ref=src, dst_ref=dst, send_sem=send, recv_sem=recv, device_id=device, device_id_type=MESH
        )

    own_copies, sends, crosses, relays = {}, {}, {}, {}
    for s in range(2):
        for p in range(2):
            src = objects[p].at[0, s]
            dst = whole[s].at[p, my_rows(m)]
            own_copies[s, p] = pltpu.make_async_copy(src, dst, tile_local.at[s, p])
            crosses[s, p] = remote(src, dst, g_send.at[0, s, p], g_recv.at[0, s, p], to_across)
            sends[s, p] = remote(src, dst, g_send.at[1, s, p], g_recv.at[1, s, p], to_sibling)
            got = whole[s].at[p, my_rows(across)]
            relays[s, p] = remote(got, got, g_send.at[2, s, p], g_recv.at[2, s, p], to_sibling)

    pl.semaphore_wait(barrier, 4)
    for s in range(2):
        for p in range(2):
            crosses[s, p].start()
    for s in range(2):
        for p in range(2):
            own_copies[s, p].start()
            sends[s, p].start()

    crop_grad[...] = jnp.zeros_like(crop_grad)
    out_probe[...] = jnp.zeros_like(out_probe)
    for load in loads:
        load.wait()
    for f in range(2):
        m_high, m_low = two_parts(measured[f])
        mixed = product(orders[0], m_high) + product(orders[0], m_low)
        m_high, m_low = two_parts(mixed)
        measured[f] = product(m_high, orders[1]) + product(m_low, orders[1])

    def tile_ready(s):
        for p in range(2):
            crosses[s, p].wait_recv()
            relays[s, p].start()
        for p in range(2):
            own_copies[s, p].wait()
            sends[s, p].wait_recv()
        for p in range(2):
            relays[s, p].wait_recv()

    row = [positions[0, f, 0] for f in range(2)]
    col = [positions[0, f, 1] for f in range(2)]

    def lines_at(lines, start, count):
        length = lines.shape[0]
        return pltpu.roll(lines, lax.rem(length - start, length), 0)[:count]

    def take_crops(s):
        for f in range(2):
            back = lax.rem(TILE - col[f], TILE)
            for p in range(2):
                lines = lines_at(whole[s][p], row[f], PX)
                crops[f, s, p] = pltpu.roll(lines, back, 1)[:, :PX]

    tile_ready(0)
    take_crops(0)

    def pass_through(step, carry):
        f, mode = step // 2, lax.rem(step, 2)
        re, im = times(probe[0, mode], probe[1, mode], crops[f, 0, 0], crops[f, 0, 1])
        re, im = both_sides(table, THROUGH, re, im)
        wave1[f, mode, 0] = re
        wave1[f, mode, 1] = im
        return carry

    lax.fori_loop(0, 4, pass_through, 0)
    tile_ready(1)
    take_crops(1)

    def far_fields(f):
        ipart[f] = jnp.zeros_like(ipart[f])

        def step(mode, carry):
            re, im = times(wave1[f, mode, 0], wave1[f, mode, 1], crops[f, 1, 0], crops[f, 1, 1])
            re, im = both_sides(table, FORTH, re, im)
            far[f, mode, 0] = re
            far[f, mode, 1] = im
            ipart[f] += re * re + im * im
            return carry

        lax.fori_loop(0, 2, step, 0)

    def half_rows(who):
        return pl.ds(pl.multiple_of(who * HALF, HALF), HALF)

    to_pair = [
        remote(ipart.at[f, half_rows(1 - core)], isib.at[f], i_send.at[0, f], i_recv.at[0, f], to_sibling) for f in range(2)
    ]
    to_other = [remote(isum.at[f], icross.at[f], i_send.at[1, f], i_recv.at[1, f], to_across) for f in range(2)]
    to_share = [
        remote(
            factor.at[f, half_rows(core)],
            factor.at[f, half_rows(core)],
            i_send.at[2, f],
            i_recv.at[2, f],
            to_sibling,
        )
        for f in range(2)
    ]

    def pair_sum(f):
        to_pair[f].wait_recv()
        isum[f] = ipart[f, half_rows(core), :] + isib[f]
        to_other[f].start()

    def factors(f):
        to_other[f].wait_recv()
        total = isum[f] + icross[f]
        factor[f, half_rows(core), :] = 2.0 - 2.0 * measured[f, half_rows(core), :] / jnp.sqrt(total + FLOOR)
        to_share[f].start()

    far_fields(0)
    to_pair[0].start()
    far_fields(1)
    to_pair[1].start()
    pair_sum(0)
    pair_sum(1)
    factors(0)

    def back_to_slice_1(f):
        def step(mode, carry):
            weight = factor[f]
            re, im = weight * far[f, mode, 0], -(weight * far[f, mode, 1])
            re, im = both_sides(table, BACK, re, im)
            gr, gi = times(wave1[f, mode, 0], wave1[f, mode, 1], re, im)
            crop_grad[f, 1, 0, EDGE : EDGE + PX, :PX] += gr
            crop_grad[f, 1, 1, EDGE : EDGE + PX, :PX] -= gi
            re, im = times(crops[f, 1, 0], crops[f, 1, 1], re, im)
            far[f, mode, 0] = re
            far[f, mode, 1] = im
            return carry

        lax.fori_loop(0, 2, step, 0)

    def back_to_probe(f):
        def step(mode, carry):
            re, im = both_sides(table, THROUGH, far[f, mode, 0], far[f, mode, 1])
            gr, gi = times(probe[0, mode], probe[1, mode], re, im)
            crop_grad[f, 0, 0, EDGE : EDGE + PX, :PX] += gr
            crop_grad[f, 0, 1, EDGE : EDGE + PX, :PX] -= gi
            gr, gi = times(crops[f, 0, 0], crops[f, 0, 1], re, im)
            out_probe[0, mode] += gr
            out_probe[1, mode] -= gi
            return carry

        lax.fori_loop(0, 2, step, 0)

    def piece(s, p, who):
        total = None
        for f in range(2):
            lines = lines_at(crop_grad[f, s, p], EDGE - row[f] + who * ROWS, ROWS)
            lines = pltpu.roll(lines, col[f], 1)
            total = lines if total is None else total + lines
        return total

    rs_pair, rs_over, rs_edge = {}, {}, {}
    for s in range(2):
        for k in range(2):
            rs_pair[s, k] = remote(rs_send.at[s, k], rs_got.at[s, k], r_send.at[k, s], r_recv.at[k, s], to_sibling)
        rs_over[s] = remote(rs_cross.at[s], rs_cross_got.at[s], r_send.at[2, s], r_recv.at[2, s], to_across)
        rs_edge[s, 0] = remote(edge_send.at[s, 0], edge_got.at[s, 0], e_send.at[0, s], e_recv.at[0, s], to_right)
        rs_edge[s, 1] = remote(edge_send.at[s, 1], edge_got.at[s, 1], e_send.at[1, s], e_recv.at[1, s], to_left)

    def reduce_start(s):
        for k, who in enumerate((diagonal, sibling)):
            for p in range(2):
                rs_send[s, k, p] = piece(s, p, who)
            rs_pair[s, k].start()
        for p in range(2):
            rs_cross[s, p] = piece(s, p, across)
        rs_pair[s, 0].wait_recv()
        for p in range(2):
            rs_cross[s, p] += rs_got[s, 0, p]
        rs_over[s].start()
        for p in range(2):
            own[s, p] = piece(s, p, m)
        rs_pair[s, 1].wait_recv()
        for p in range(2):
            own[s, p] += rs_got[s, 1, p]

    lane = lax.broadcasted_iota(jnp.int32, (ROWS, 128), 1)
    lower = lane < MARGIN

    def reduce_middle(s):
        rs_over[s].wait_recv()
        for p in range(2):
            own[s, p] += rs_cross_got[s, p]
        last = (own[s, 0, :, TILE - 128 :], own[s, 1, :, TILE - 128 :])
        first = (own[s, 0, :, :128], own[s, 1, :, :128])
        edge_send[s, 0] = jnp.where(lower, pltpu.roll(last[0], MARGIN, 1), last[1])
        edge_send[s, 1] = jnp.where(lower, first[0], pltpu.roll(first[1], MARGIN, 1))
        rs_edge[s, 0].start()
        rs_edge[s, 1].start()

    def reduce_end(s):
        rs_edge[s, 0].wait_recv()
        rs_edge[s, 1].wait_recv()
        before, after = edge_got[s, 0], edge_got[s, 1]
        at_first = jnp.logical_and(lower, t > 0)
        at_last = jnp.logical_and(jnp.logical_not(lower), t < tiles - 1)
        outs = (out_re, out_im)
        befores = (before, pltpu.roll(before, MARGIN, 1))
        afters = (pltpu.roll(after, MARGIN, 1), after)
        for p in range(2):
            out = outs[p]
            out[0, s, :, :128] = own[s, p, :, :128] + jnp.where(at_first, befores[p], 0.0)
            out[0, s, :, 128 : TILE - 128] = own[s, p, :, 128 : TILE - 128]
            out[0, s, :, TILE - 128 :] = own[s, p, :, TILE - 128 :] + jnp.where(at_last, afters[p], 0.0)

    to_share[0].wait_recv()
    back_to_slice_1(0)
    back_to_probe(0)
    factors(1)
    to_share[1].wait_recv()
    back_to_slice_1(1)
    reduce_start(1)
    back_to_probe(1)
    reduce_start(0)
    reduce_middle(1)
    reduce_middle(0)
    reduce_end(1)
    reduce_end(0)

    for group in (sends, crosses, relays, rs_pair, rs_over, rs_edge):
        for copy in group.values():
            copy.wait_send()
    for group in (to_pair, to_other, to_share):
        for copy in group:
            copy.wait_send()


def gradients(obj_re, obj_im, probe, measured, positions, table, orders):
    tiles = lax.axis_size("tile")
    shape = jax.ShapeDtypeStruct
    anywhere = pl.BlockSpec(memory_space=pl.ANY)
    vmem = pl.BlockSpec(memory_space=pltpu.VMEM)
    return pl.pallas_call(
        functools.partial(kernel, tiles),
        out_shape=(shape(obj_re.shape, F32), shape(obj_im.shape, F32), shape(probe.shape, F32)),
        in_specs=[anywhere, anywhere, anywhere, anywhere, pl.BlockSpec(memory_space=pltpu.SMEM), anywhere, anywhere],
        out_specs=(vmem, vmem, vmem),
        scratch_shapes=[
            pltpu.VMEM((2, TILE, TILE), F32),
            pltpu.VMEM((2, TILE, TILE), F32),
            pltpu.VMEM((2, 2, 2, PX, PX), F32),
            pltpu.VMEM((2, 2, PX, PX), F32),
            pltpu.VMEM((2, PX, PX), F32),
            pltpu.VMEM(table.shape, BF16),
            pltpu.VMEM(orders.shape, BF16),
            pltpu.VMEM((2, 2, 2, PX, PX), F32),
            pltpu.VMEM((2, 2, 2, PX, PX), F32),
            pltpu.VMEM((2, PX, PX), F32),
            pltpu.VMEM((2, HALF, PX), F32),
            pltpu.VMEM((2, HALF, PX), F32),
            pltpu.VMEM((2, HALF, PX), F32),
            pltpu.VMEM((2, PX, PX), F32),
            pltpu.VMEM((2, 2, 2, PX + 2 * EDGE, TILE), F32),
            pltpu.VMEM((2, 2, 2, ROWS, TILE), F32),
            pltpu.VMEM((2, 2, 2, ROWS, TILE), F32),
            pltpu.VMEM((2, 2, ROWS, TILE), F32),
            pltpu.VMEM((2, 2, ROWS, TILE), F32),
            pltpu.VMEM((2, 2, ROWS, TILE), F32),
            pltpu.VMEM((2, 2, ROWS, 128), F32),
            pltpu.VMEM((2, 2, ROWS, 128), F32),
            pltpu.SemaphoreType.DMA((4,)),
            pltpu.SemaphoreType.DMA((2, 2)),
            pltpu.SemaphoreType.DMA((3, 2, 2)),
            pltpu.SemaphoreType.DMA((3, 2, 2)),
            pltpu.SemaphoreType.DMA((3, 2)),
            pltpu.SemaphoreType.DMA((3, 2)),
            pltpu.SemaphoreType.DMA((3, 2)),
            pltpu.SemaphoreType.DMA((3, 2)),
            pltpu.SemaphoreType.DMA((2, 2)),
            pltpu.SemaphoreType.DMA((2, 2)),
        ],
        compiler_params=pltpu.CompilerParams(
            collective_id=0, has_side_effects=True, vmem_limit_bytes=56 * 1024 * 1024
        ),
        cost_estimate=pl.CostEstimate(flops=7 * 10**9, bytes_accessed=10**7, transcendentals=10**6),
    )(obj_re, obj_im, probe, measured, positions, table, orders)


def total_of(shard, axis):
    count = lax.axis_size(axis)
    lines = shard.reshape(count, -1, shard.shape[-1])
    tiles = lax.all_to_all(lines, axis, 0, 0, tiled=True)
    own = jnp.sum(tiles, axis=0)
    copies = jnp.broadcast_to(own, (count, *own.shape))
    return lax.all_to_all(copies, axis, 0, 0, tiled=True).reshape(shard.shape)


def body(object_real, object_imag, probe, measured, positions):
    table, orders = constants()
    grad_re, grad_im, probe_part = gradients(
        object_real, object_imag, probe, measured, positions, jnp.asarray(table), jnp.asarray(orders)
    )
    return grad_re, grad_im, total_of(probe_part, "tile")


def solution(mesh):
    return jax.shard_map(
        body,
        mesh=mesh,
        in_specs=(
            P("tile", None, "mode", None),
            P("tile", None, "mode", None),
            P(None, "mode", None, None),
            P("tile", None, None, None),
            P("tile", None, None),
        ),
        out_specs=(
            P("tile", None, "mode", None),
            P("tile", None, "mode", None),
            P(None, "mode", None, None),
        ),
        check_vma=False,
    )
```

profile of v0, /device:TPU:0, one launch (start us, length us, event | category | flops | bytes accessed | tf_op | source)
XLA Modules:
  0.0 119.2 jit_solution(12524986096186490303)
XLA Ops:
  0.6 68.4 %shard_map.94 = (f32[1,2,96,384]{3,2,1,0:T(8,128)}, f32[1,2,96,384]{3,2,1,0:T(8,128)}, f32[2,2,256,256]{3,2,1,0:T(8,128)}) custom-call(f32[1,2,96,384]{3,2,1,0:T(8,128)} %obj_re.1, f32[1,2,96,384]{3,2,1,0:T(8,128)} %obj_im.1, f32[2,2,256,256]{3,2,1,0:T(8,128)} %probe_in.1, f32[1,2,256,256]{3,2,1,0:T(8,128)} %measured_in.1, s32[1,2,2]{2,1,0:T(2,128)} %positions.1, ...), custom_call_target="tpu_custom_call" | custom-call | flops 7000000000 | bytes 10000000 | tf_op jit(solution)/shard_map/pallas_call | solution.py:439
  69.1 0.0 copy-start.1
  69.1 0.0 copy-start
  69.1 24.5 %all_to_all.10 = f32[32,32,256]{2,1,0:T(8,128)S(1)} all-to-all(f32[32,32,256]{2,1,0:T(8,128)} %bitcast.3), channel_id=1, replica_groups=mesh['tile'=32,'mode'=4] {'tile'}, dimensions={0} | all-to-all | bytes 2097152 | tf_op jit(solution)/shard_map/all_to_all | solution.py:488
  93.6 0.1 reduce_sum.9
  93.6 1.1 broadcast_in_dim.3
  94.7 4.5 %all-to-all-start.1 = ((f32[32,32,256]{2,1,0:T(8,128)}), f32[32,32,256]{2,1,0:T(8,128)S(1)}, u32[]{:S(2)}, u32[]{:S(2)}) async-start(f32[32,32,256]{2,1,0:T(8,128)} %broadcast_in_dim.3), calls=%async_computation.1 | async-start | bytes 2097152 | tf_op jit(solution)/shard_map/all_to_all | solution.py:491
  99.2 17.6 %all-to-all-done.1 = f32[32,32,256]{2,1,0:T(8,128)S(1)} async-done(((f32[32,32,256]{2,1,0:T(8,128)}), f32[32,32,256]{2,1,0:T(8,128)S(1)}, u32[]{:S(2)}, u32[]{:S(2)}) %all-to-all-start.1) | async-done | bytes 1048608 | tf_op jit(solution)/shard_map/all_to_all | solution.py:491
  116.8 0.0 copy-done.1
  116.8 0.7 copy.13
  117.5 0.0 copy-done
  117.5 0.7 copy.14
  118.2 1.0 copy.15
Async XLA Ops:
  69.1 47.7 %copy-start.1 = (f32[1,2,96,384]{3,2,1,0:T(8,128)S(1)}, f32[1,2,96,384]{3,2,1,0:T(8,128)}, u32[]{:S(2)}) copy-start(f32[1,2,96,384]{3,2,1,0:T(8,128)} %get-tuple-element.12) | copy-start | bytes 884740
  69.1 48.4 %copy-start = (f32[1,2,96,384]{3,2,1,0:T(8,128)S(1)}, f32[1,2,96,384]{3,2,1,0:T(8,128)}, u32[]{:S(2)}) copy-start(f32[1,2,96,384]{3,2,1,0:T(8,128)} %get-tuple-element.13) | copy-start | bytes 884740
  94.7 22.1 %all-to-all-start.1 = ((f32[32,32,256]{2,1,0:T(8,128)}), f32[32,32,256]{2,1,0:T(8,128)S(1)}, u32[]{:S(2)}, u32[]{:S(2)}) async-start(f32[32,32,256]{2,1,0:T(8,128)} %broadcast_in_dim.3), calls=%async_computation.1 | async-start | bytes 2097152 | tf_op jit(solution)/shard_map/all_to_all | solution.py:491
where the time goes:
time: 120 us; the launch traced here: 119 us
  Pallas kernels  68.4 us (57%)
  blocking collectives  24.5 us (20%)
  waiting for transfers between devices  17.6 us (15%)
  starting transfers between devices  4.47 us (4%)
  local copies, waits for them, and re-layouts  3.5 us (3%)
    pallas_call x1, Pallas kernels, gradients(): pl.pallas_call(functools.partial(kernel, tiles), out_shape=(shape(obj_re....  68.4 us
    all_to_all x1, blocking collectives, total_of(): tiles = lax.all_to_all(lines, axis, 0, 0, tiled=True)  24.5 us
    all_to_all x1, waiting for transfers between devices, total_of(): return lax.all_to_all(copies, axis, 0, 0, tiled=True).reshape(shard.shape)  17.6 us
    all_to_all x1, starting transfers between devices, total_of(): return lax.all_to_all(copies, axis, 0, 0, tiled=True).reshape(shard.shape)  4.47 us
    unnamed x7, local copies, waits for them, and re-layouts  2.41 us
  transfers between devices with their start and end apart: 1, of which 1 were waited for; matrix products, arithmetic and copies ran while one was open for 0% of the time, Pallas kernels for 0%

commit v1 on v0

--- a/solution.py
+++ b/solution.py
@@ -146,6 +146,7 @@
     icross,
     factor,
     crop_grad,
+    tile_grad,
     rs_send,
     rs_got,
     rs_cross,
@@ -163,6 +164,14 @@
     r_recv,
     e_send,
     e_recv,
+    partial,
+    got_a,
+    got_b,
+    part_b,
+    y_send_buf,
+    y_got,
+    p_send,
+    p_recv,
 ):
     t = lax.axis_index("tile")
     m = lax.axis_index("mode")
@@ -176,8 +185,14 @@
     to_sibling, to_across = (t, sibling), (t, across)
     to_left, to_right = (left, m), (right, m)
 
+    ring = 4
+    tz, ty, tx = lax.rem(t, ring), lax.rem(t // ring, 2), t // (2 * ring)
+    z_peers = [(t - tz + lax.rem(tz + d, ring), m) for d in range(1, ring)]
+    x_peers = [(lax.rem(t + 2 * ring * d, tiles), m) for d in range(1, ring)]
+    y_peer = (t + ring * (1 - 2 * ty), m)
+
     barrier = pltpu.get_barrier_semaphore()
-    for device in (to_sibling, to_across, to_left, to_right):
+    for device in (to_sibling, to_across, to_left, to_right, y_peer, *z_peers, *x_peers):
         pl.semaphore_signal(barrier, inc=1, device_id=device, device_id_type=MESH)
 
     loads = [
@@ -211,7 +226,7 @@
             got = whole[s].at[p, my_rows(across)]
             relays[s, p] = remote(got, got, g_send.at[2, s, p], g_recv.at[2, s, p], to_sibling)
 
-    pl.semaphore_wait(barrier, 4)
+    pl.semaphore_wait(barrier, 11)
     for s in range(2):
         for p in range(2):
             crosses[s, p].start()
@@ -221,7 +236,7 @@
             sends[s, p].start()
 
     crop_grad[...] = jnp.zeros_like(crop_grad)
-    out_probe[...] = jnp.zeros_like(out_probe)
+    partial[...] = jnp.zeros_like(partial)
     for load in loads:
         load.wait()
     for f in range(2):
@@ -243,15 +258,11 @@
     row = [positions[0, f, 0] for f in range(2)]
     col = [positions[0, f, 1] for f in range(2)]
 
-    def lines_at(lines, start, count):
-        length = lines.shape[0]
-        return pltpu.roll(lines, lax.rem(length - start, length), 0)[:count]
-
     def take_crops(s):
         for f in range(2):
-            back = lax.rem(TILE - col[f], TILE)
+            up, back = lax.rem(TILE - row[f], TILE), lax.rem(TILE - col[f], TILE)
             for p in range(2):
-                lines = lines_at(whole[s][p], row[f], PX)
+                lines = pltpu.roll(whole[s][p], up, 0)[:PX]
                 crops[f, s, p] = pltpu.roll(lines, back, 1)[:, :PX]
 
     tile_ready(0)
@@ -325,8 +336,8 @@
             re, im = weight * far[f, mode, 0], -(weight * far[f, mode, 1])
             re, im = both_sides(table, BACK, re, im)
             gr, gi = times(wave1[f, mode, 0], wave1[f, mode, 1], re, im)
-            crop_grad[f, 1, 0, EDGE : EDGE + PX, :PX] += gr
-            crop_grad[f, 1, 1, EDGE : EDGE + PX, :PX] -= gi
+            crop_grad[f, 1, 0] += gr
+            crop_grad[f, 1, 1] -= gi
             re, im = times(crops[f, 1, 0], crops[f, 1, 1], re, im)
             far[f, mode, 0] = re
             far[f, mode, 1] = im
@@ -334,26 +345,36 @@
 
         lax.fori_loop(0, 2, step, 0)
 
-    def back_to_probe(f):
-        def step(mode, carry):
+    def back_to_probe(steps):
+        def step(k, carry):
+            f, mode = steps[0][0], steps[0][1]
+            if len(steps) > 1:
+                f = f + k * (steps[1][0] - f)
+                mode = mode + k * (steps[1][1] - mode)
             re, im = both_sides(table, THROUGH, far[f, mode, 0], far[f, mode, 1])
             gr, gi = times(probe[0, mode], probe[1, mode], re, im)
-            crop_grad[f, 0, 0, EDGE : EDGE + PX, :PX] += gr
-            crop_grad[f, 0, 1, EDGE : EDGE + PX, :PX] -= gi
+            crop_grad[f, 0, 0] += gr
+            crop_grad[f, 0, 1] -= gi
             gr, gi = times(crops[f, 0, 0], crops[f, 0, 1], re, im)
-            out_probe[0, mode] += gr
-            out_probe[1, mode] -= gi
+            partial[mode, 0] += gr
+            partial[mode, 1] -= gi
             return carry
 
-        lax.fori_loop(0, 2, step, 0)
+        lax.fori_loop(0, len(steps), step, 0)
+
+    def place(s):
+        for p in range(2):
+            total = None
+            for f in range(2):
+                wide = jnp.concatenate([crop_grad[f, s, p], jnp.zeros((PX, EDGE), F32)], axis=1)
+                wide = pltpu.roll(wide, col[f], 1)
+                wide = jnp.concatenate([wide, jnp.zeros((EDGE, TILE), F32)], axis=0)
+                wide = pltpu.roll(wide, row[f], 0)
+                total = wide if total is None else total + wide
+            tile_grad[s, p] = total
 
     def piece(s, p, who):
-        total = None
-        for f in range(2):
-            lines = lines_at(crop_grad[f, s, p], EDGE - row[f] + who * ROWS, ROWS)
-            lines = pltpu.roll(lines, col[f], 1)
-            total = lines if total is None else total + lines
-        return total
+        return tile_grad[s, p, my_rows(who), :]
 
     rs_pair, rs_over, rs_edge = {}, {}, {}
     for s in range(2):
@@ -364,6 +385,7 @@
         rs_edge[s, 1] = remote(edge_send.at[s, 1], edge_got.at[s, 1], e_send.at[1, s], e_recv.at[1, s], to_left)
 
     def reduce_start(s):
+        place(s)
         for k, who in enumerate((diagonal, sibling)):
             for p in range(2):
                 rs_send[s, k, p] = piece(s, p, who)
@@ -409,20 +431,95 @@
             out[0, s, :, 128 : TILE - 128] = own[s, p, :, 128 : TILE - 128]
             out[0, s, :, TILE - 128 :] = own[s, p, :, TILE - 128 :] + jnp.where(at_last, afters[p], 0.0)
 
+    axes = (((tz, z_peers), (tx, x_peers)), ((tx, x_peers), (tz, z_peers)))
+
+    def block(length, index, base=0):
+        return pl.ds(pl.multiple_of(base + index * length, length), length)
+
+    scatter_a, scatter_b, swap_y, gather_b, gather_a = {}, {}, {}, {}, {}
+    for c in range(2):
+        (ia, peers_a), (ib, peers_b) = axes[c]
+        for d in range(1, ring):
+            k = d - 1
+            ja, jb = lax.rem(ia + d, ring), lax.rem(ib + d, ring)
+            scatter_a[c, k] = remote(
+                partial.at[c, :, block(64, ja)], got_a.at[c, k], p_send.at[c, 0, k], p_recv.at[c, 0, k], peers_a[k]
+            )
+            scatter_b[c, k] = remote(
+                part_b.at[c, :, block(16, jb)], got_b.at[c, k], p_send.at[c, 1, k], p_recv.at[c, 1, k], peers_b[k]
+            )
+            mine_b = out_probe.at[:, c, block(16, ib, ia * 64)]
+            gather_b[c, k] = remote(mine_b, mine_b, p_send.at[c, 2, k], p_recv.at[c, 2, k], peers_b[k])
+            mine_a = out_probe.at[:, c, block(64, ia)]
+            gather_a[c, k] = remote(mine_a, mine_a, p_send.at[c, 3, k], p_recv.at[c, 3, k], peers_a[k])
+        swap_y[c] = remote(y_send_buf.at[c], y_got.at[c], p_send.at[c, 4, 0], p_recv.at[c, 4, 0], y_peer)
+
+    def probe_1(c):
+        for k in (1, 0, 2):
+            scatter_a[c, k].start()
+
+    def probe_2(c):
+        ia = axes[c][0][0]
+        for k in range(3):
+            scatter_a[c, k].wait_recv()
+        part_b[c] = partial[c, :, block(64, ia), :] + got_a[c, 0] + got_a[c, 1] + got_a[c, 2]
+        for k in (1, 0, 2):
+            scatter_b[c, k].start()
+
+    def probe_3(c):
+        ib = axes[c][1][0]
+        for k in range(3):
+            scatter_b[c, k].wait_recv()
+        y_send_buf[c] = part_b[c, :, block(16, ib), :] + got_b[c, 0] + got_b[c, 1] + got_b[c, 2]
+        swap_y[c].start()
+
+    def probe_4(c):
+        ia, ib = axes[c][0][0], axes[c][1][0]
+        swap_y[c].wait_recv()
+        out_probe[:, c, block(16, ib, ia * 64), :] = y_send_buf[c] + y_got[c]
+        for k in (1, 0, 2):
+            gather_b[c, k].start()
+
+    def probe_5(c):
+        for k in range(3):
+            gather_b[c, k].wait_recv()
+        for k in (1, 0, 2):
+            gather_a[c, k].start()
+
+    def probe_6(c):
+        for k in range(3):
+            gather_a[c, k].wait_recv()
+
     to_share[0].wait_recv()
     back_to_slice_1(0)
-    back_to_probe(0)
+    back_to_probe([(0, 0)])
     factors(1)
     to_share[1].wait_recv()
     back_to_slice_1(1)
     reduce_start(1)
-    back_to_probe(1)
+    back_to_probe([(1, 0)])
+    probe_1(0)
+    back_to_probe([(0, 1), (1, 1)])
+    probe_1(1)
+    probe_2(0)
     reduce_start(0)
+    probe_2(1)
+    probe_3(0)
     reduce_middle(1)
+    probe_3(1)
+    probe_4(0)
     reduce_middle(0)
+    probe_4(1)
+    probe_5(0)
     reduce_end(1)
+    probe_5(1)
     reduce_end(0)
-
+    probe_6(0)
+    probe_6(1)
+
+    for group in (scatter_a, scatter_b, swap_y, gather_b, gather_a):
+        for copy in group.values():
+            copy.wait_send()
     for group in (sends, crosses, relays, rs_pair, rs_over, rs_edge):
         for copy in group.values():
             copy.wait_send()
@@ -456,7 +553,8 @@
             pltpu.VMEM((2, HALF, PX), F32),
             pltpu.VMEM((2, HALF, PX), F32),
             pltpu.VMEM((2, PX, PX), F32),
-            pltpu.VMEM((2, 2, 2, PX + 2 * EDGE, TILE), F32),
+            pltpu.VMEM((2, 2, 2, PX, PX), F32),
+            pltpu.VMEM((2, 2, TILE, TILE), F32),
             pltpu.VMEM((2, 2, 2, ROWS, TILE), F32),
             pltpu.VMEM((2, 2, 2, ROWS, TILE), F32),
             pltpu.VMEM((2, 2, ROWS, TILE), F32),
@@ -474,6 +572,14 @@
             pltpu.SemaphoreType.DMA((3, 2)),
             pltpu.SemaphoreType.DMA((2, 2)),
             pltpu.SemaphoreType.DMA((2, 2)),
+            pltpu.VMEM((2, 2, PX, PX), F32),
+            pltpu.VMEM((2, 3, 2, 64, PX), F32),
+            pltpu.VMEM((2, 3, 2, 16, PX), F32),
+            pltpu.VMEM((2, 2, 64, PX), F32),
+            pltpu.VMEM((2, 2, 16, PX), F32),
+            pltpu.VMEM((2, 2, 16, PX), F32),
+            pltpu.SemaphoreType.DMA((2, 5, 3)),
+            pltpu.SemaphoreType.DMA((2, 5, 3)),
         ],
         compiler_params=pltpu.CompilerParams(
             collective_id=0, has_side_effects=True, vmem_limit_bytes=56 * 1024 * 1024
@@ -482,21 +588,9 @@
     )(obj_re, obj_im, probe, measured, positions, table, orders)
 
 
-def total_of(shard, axis):
-    count = lax.axis_size(axis)
-    lines = shard.reshape(count, -1, shard.shape[-1])
-    tiles = lax.all_to_all(lines, axis, 0, 0, tiled=True)
-    own = jnp.sum(tiles, axis=0)
-    copies = jnp.broadcast_to(own, (count, *own.shape))
-    return lax.all_to_all(copies, axis, 0, 0, tiled=True).reshape(shard.shape)
-
-
 def body(object_real, object_imag, probe, measured, positions):
     table, orders = constants()
-    grad_re, grad_im, probe_part = gradients(
-        object_real, object_imag, probe, measured, positions, jnp.asarray(table), jnp.asarray(orders)
-    )
-    return grad_re, grad_im, total_of(probe_part, "tile")
+    return gradients(object_real, object_imag, probe, measured, positions, jnp.asarray(table), jnp.asarray(orders))
 
 
 def solution(mesh):

time: 120 us -> 87.4 us (0.73)
  blocking collectives: 24.5 us -> 0 us
  waiting for transfers between devices: 17.6 us -> 0 us
  Pallas kernels: 68.4 us -> 80.7 us
  starting transfers between devices: 4.47 us -> 0 us
  local copies, waits for them, and re-layouts: 3.5 us -> 5.67 us
    all_to_all x1 -> x0, blocking collectives: 24.5 us -> none  [total_of(): tiles = lax.all_to_all(lines, axis, 0, 0, tiled=True)]
    all_to_all x1 -> x0, waiting for transfers between devices: 17.6 us -> none  [total_of(): return lax.all_to_all(copies, axis, 0, 0, tiled=True).reshape(shard.shape)]
    pallas_call x1, Pallas kernels: 68.4 us -> 80.7 us  [gradients(): pl.pallas_call(functools.partial(kernel, tiles), out_shape=(shape(obj_re....]
    all_to_all x1 -> x0, starting transfers between devices: 4.47 us -> none  [total_of(): return lax.all_to_all(copies, axis, 0, 0, tiled=True).reshape(shard.shape)]
    unnamed x7 -> x3, local copies, waits for them, and re-layouts: 2.41 us -> 5.67 us
  transfers between devices with their start and end apart: 1 -> 0, of which waited for: 1 -> 0; matrix products, arithmetic and copies ran while one was open for 0% -> 0% of each run, Pallas kernels for 0% -> 0%
where the time goes in v1:
time: 87.4 us; the launch traced here: 87 us
  Pallas kernels  80.7 us (92%)
  local copies, waits for them, and re-layouts  5.67 us (6%)
    pallas_call x1, Pallas kernels, gradients(): pl.pallas_call(functools.partial(kernel, tiles), out_shape=(shape(obj_re....  80.7 us
    unnamed x3, local copies, waits for them, and re-layouts  5.67 us

profile of v1, /device:TPU:0, one launch (start us, length us, event | category | flops | bytes accessed | tf_op | source)
XLA Modules:
  0.0 87.0 jit_solution(15788620435306879912)
XLA Ops:
  0.6 80.7 %shard_map.94 = (f32[1,2,96,384]{3,2,1,0:T(8,128)}, f32[1,2,96,384]{3,2,1,0:T(8,128)}, f32[2,2,256,256]{3,2,1,0:T(8,128)}) custom-call(f32[1,2,96,384]{3,2,1,0:T(8,128)} %obj_re.1, f32[1,2,96,384]{3,2,1,0:T(8,128)} %obj_im.1, f32[2,2,256,256]{3,2,1,0:T(8,128)} %probe_in.1, f32[1,2,256,256]{3,2,1,0:T(8,128)} %measured_in.1, s32[1,2,2]{2,1,0:T(2,128)} %positions.1, ...), custom_call_target="tpu_custom_call" | custom-call | flops 7000000000 | bytes 10000000 | tf_op jit(solution)/shard_map/pallas_call | solution.py:536
  81.3 1.7 %copy.13 = f32[1,2,96,384]{3,2,1,0:T(8,128)} copy(f32[1,2,96,384]{3,2,1,0:T(8,128)} %get-tuple-element.6) | data formatting | bytes 589824
  83.0 1.7 %copy.14 = f32[1,2,96,384]{3,2,1,0:T(8,128)} copy(f32[1,2,96,384]{3,2,1,0:T(8,128)} %get-tuple-element.7) | data formatting | bytes 589824
  84.7 2.3 %copy.15 = f32[2,2,256,256]{3,2,1,0:T(8,128)} copy(f32[2,2,256,256]{3,2,1,0:T(8,128)} %get-tuple-element.8) | data formatting | bytes 2097152

commit v2 on v1

--- a/solution.py
+++ b/solution.py
@@ -172,6 +172,9 @@
     y_got,
     p_send,
     p_recv,
+    total,
+    out_sem,
+    probe_sem,
 ):
     t = lax.axis_index("tile")
     m = lax.axis_index("mode")
@@ -318,8 +321,8 @@
 
     def factors(f):
         to_other[f].wait_recv()
-        total = isum[f] + icross[f]
-        factor[f, half_rows(core), :] = 2.0 - 2.0 * measured[f, half_rows(core), :] / jnp.sqrt(total + FLOOR)
+        whole_sum = isum[f] + icross[f]
+        factor[f, half_rows(core), :] = 2.0 - 2.0 * measured[f, half_rows(core), :] / jnp.sqrt(whole_sum + FLOOR)
         to_share[f].start()
 
     far_fields(0)
@@ -330,85 +333,98 @@
     pair_sum(1)
     factors(0)
 
-    def back_to_slice_1(f):
-        def step(mode, carry):
-            weight = factor[f]
-            re, im = weight * far[f, mode, 0], -(weight * far[f, mode, 1])
-            re, im = both_sides(table, BACK, re, im)
-            gr, gi = times(wave1[f, mode, 0], wave1[f, mode, 1], re, im)
-            crop_grad[f, 1, 0] += gr
-            crop_grad[f, 1, 1] -= gi
-            re, im = times(crops[f, 1, 0], crops[f, 1, 1], re, im)
-            far[f, mode, 0] = re
-            far[f, mode, 1] = im
-            return carry
-
-        lax.fori_loop(0, 2, step, 0)
-
-    def back_to_probe(steps):
+    def over(steps, body):
         def step(k, carry):
-            f, mode = steps[0][0], steps[0][1]
+            f, mode = steps[0]
             if len(steps) > 1:
                 f = f + k * (steps[1][0] - f)
                 mode = mode + k * (steps[1][1] - mode)
-            re, im = both_sides(table, THROUGH, far[f, mode, 0], far[f, mode, 1])
-            gr, gi = times(probe[0, mode], probe[1, mode], re, im)
-            crop_grad[f, 0, 0] += gr
-            crop_grad[f, 0, 1] -= gi
-            gr, gi = times(crops[f, 0, 0], crops[f, 0, 1], re, im)
-            partial[mode, 0] += gr
-            partial[mode, 1] -= gi
+            body(f, mode)
             return carry
 
         lax.fori_loop(0, len(steps), step, 0)
 
+    def slice_1_step(f, mode):
+        weight = factor[f]
+        re, im = weight * far[f, mode, 0], -(weight * far[f, mode, 1])
+        re, im = both_sides(table, BACK, re, im)
+        gr, gi = times(wave1[f, mode, 0], wave1[f, mode, 1], re, im)
+        crop_grad[f, 1, 0] += gr
+        crop_grad[f, 1, 1] -= gi
+        re, im = times(crops[f, 1, 0], crops[f, 1, 1], re, im)
+        far[f, mode, 0] = re
+        far[f, mode, 1] = im
+
+    def probe_step(f, mode):
+        re, im = both_sides(table, THROUGH, far[f, mode, 0], far[f, mode, 1])
+        gr, gi = times(probe[0, mode], probe[1, mode], re, im)
+        crop_grad[f, 0, 0] += gr
+        crop_grad[f, 0, 1] -= gi
+        gr, gi = times(crops[f, 0, 0], crops[f, 0, 1], re, im)
+        partial[mode, 0] += gr
+        partial[mode, 1] -= gi
+
+    def both_steps(f, mode):
+        slice_1_step(f, mode)
+        probe_step(f, mode)
+
     def place(s):
         for p in range(2):
-            total = None
+            placed = None
             for f in range(2):
                 wide = jnp.concatenate([crop_grad[f, s, p], jnp.zeros((PX, EDGE), F32)], axis=1)
                 wide = pltpu.roll(wide, col[f], 1)
                 wide = jnp.concatenate([wide, jnp.zeros((EDGE, TILE), F32)], axis=0)
                 wide = pltpu.roll(wide, row[f], 0)
-                total = wide if total is None else total + wide
-            tile_grad[s, p] = total
+                placed = wide if placed is None else placed + wide
+            tile_grad[s, p] = placed
 
     def piece(s, p, who):
         return tile_grad[s, p, my_rows(who), :]
 
-    rs_pair, rs_over, rs_edge = {}, {}, {}
+    parts = (pl.ds(0, 128), pl.ds(TILE - 128, 128), pl.ds(128, TILE - 256))
+    rs_pair, rs_over, rs_edge, outward = {}, {}, {}, {}
     for s in range(2):
         for k in range(2):
             rs_pair[s, k] = remote(rs_send.at[s, k], rs_got.at[s, k], r_send.at[k, s], r_recv.at[k, s], to_sibling)
-        rs_over[s] = remote(rs_cross.at[s], rs_cross_got.at[s], r_send.at[2, s], r_recv.at[2, s], to_across)
+        for k in range(3):
+            rs_over[s, k] = remote(
+                rs_cross.at[s, :, :, parts[k]],
+                rs_cross_got.at[s, :, :, parts[k]],
+                r_send.at[2 + k, s],
+                r_recv.at[2 + k, s],
+                to_across,
+            )
         rs_edge[s, 0] = remote(edge_send.at[s, 0], edge_got.at[s, 0], e_send.at[0, s], e_recv.at[0, s], to_right)
         rs_edge[s, 1] = remote(edge_send.at[s, 1], edge_got.at[s, 1], e_send.at[1, s], e_recv.at[1, s], to_left)
-
-    def reduce_start(s):
+        for p in range(2):
+            outward[s, p] = pltpu.make_async_copy(own.at[s, p], (out_re, out_im)[p].at[0, s], out_sem.at[s, p])
+
+    def reduce_1(s):
         place(s)
         for k, who in enumerate((diagonal, sibling)):
             for p in range(2):
                 rs_send[s, k, p] = piece(s, p, who)
             rs_pair[s, k].start()
-        for p in range(2):
-            rs_cross[s, p] = piece(s, p, across)
+
+    def reduce_2(s):
         rs_pair[s, 0].wait_recv()
         for p in range(2):
-            rs_cross[s, p] += rs_got[s, 0, p]
-        rs_over[s].start()
-        for p in range(2):
-            own[s, p] = piece(s, p, m)
+            rs_cross[s, p] = piece(s, p, across) + rs_got[s, 0, p]
+        for k in range(3):
+            rs_over[s, k].start()
         rs_pair[s, 1].wait_recv()
         for p in range(2):
-            own[s, p] += rs_got[s, 1, p]
+            own[s, p] = piece(s, p, m) + rs_got[s, 1, p]
 
     lane = lax.broadcasted_iota(jnp.int32, (ROWS, 128), 1)
     lower = lane < MARGIN
 
-    def reduce_middle(s):
-        rs_over[s].wait_recv()
-        for p in range(2):
-            own[s, p] += rs_cross_got[s, p]
+    def reduce_3(s):
+        for k in range(2):
+            rs_over[s, k].wait_recv()
+            for p in range(2):
+                own[s, p, :, parts[k]] += rs_cross_got[s, p, :, parts[k]]
         last = (own[s, 0, :, TILE - 128 :], own[s, 1, :, TILE - 128 :])
         first = (own[s, 0, :, :128], own[s, 1, :, :128])
         edge_send[s, 0] = jnp.where(lower, pltpu.roll(last[0], MARGIN, 1), last[1])
@@ -416,107 +432,113 @@
         rs_edge[s, 0].start()
         rs_edge[s, 1].start()
 
-    def reduce_end(s):
+    def reduce_4(s):
+        rs_over[s, 2].wait_recv()
+        for p in range(2):
+            own[s, p, :, parts[2]] += rs_cross_got[s, p, :, parts[2]]
         rs_edge[s, 0].wait_recv()
         rs_edge[s, 1].wait_recv()
         before, after = edge_got[s, 0], edge_got[s, 1]
         at_first = jnp.logical_and(lower, t > 0)
         at_last = jnp.logical_and(jnp.logical_not(lower), t < tiles - 1)
-        outs = (out_re, out_im)
         befores = (before, pltpu.roll(before, MARGIN, 1))
         afters = (pltpu.roll(after, MARGIN, 1), after)
         for p in range(2):
-            out = outs[p]
-            out[0, s, :, :128] = own[s, p, :, :128] + jnp.where(at_first, befores[p], 0.0)
-            out[0, s, :, 128 : TILE - 128] = own[s, p, :, 128 : TILE - 128]
-            out[0, s, :, TILE - 128 :] = own[s, p, :, TILE - 128 :] + jnp.where(at_last, afters[p], 0.0)
+            own[s, p, :, parts[0]] += jnp.where(at_first, befores[p], 0.0)
+            own[s, p, :, parts[1]] += jnp.where(at_last, afters[p], 0.0)
+            outward[s, p].start()
 
     axes = (((tz, z_peers), (tx, x_peers)), ((tx, x_peers), (tz, z_peers)))
 
     def block(length, index, base=0):
         return pl.ds(pl.multiple_of(base + index * length, length), length)
 
-    scatter_a, scatter_b, swap_y, gather_b, gather_a = {}, {}, {}, {}, {}
-    for c in range(2):
+    scatter_a, scatter_b, swap_y, gather_b, gather_a, probe_out = {}, {}, {}, {}, {}, {}
+    chunks = range(2)
+    for c in chunks:
         (ia, peers_a), (ib, peers_b) = axes[c]
-        for d in range(1, ring):
-            k = d - 1
-            ja, jb = lax.rem(ia + d, ring), lax.rem(ib + d, ring)
+        for k in range(ring - 1):
+            ja, jb = lax.rem(ia + k + 1, ring), lax.rem(ib + k + 1, ring)
+            sems = [(p_send.at[c, i, k], p_recv.at[c, i, k]) for i in range(4)]
             scatter_a[c, k] = remote(
-                partial.at[c, :, block(64, ja)], got_a.at[c, k], p_send.at[c, 0, k], p_recv.at[c, 0, k], peers_a[k]
+                partial.at[c, :, block(64, ja)], got_a.at[c, k], *sems[0], peers_a[k]
             )
-            scatter_b[c, k] = remote(
-                part_b.at[c, :, block(16, jb)], got_b.at[c, k], p_send.at[c, 1, k], p_recv.at[c, 1, k], peers_b[k]
-            )
-            mine_b = out_probe.at[:, c, block(16, ib, ia * 64)]
-            gather_b[c, k] = remote(mine_b, mine_b, p_send.at[c, 2, k], p_recv.at[c, 2, k], peers_b[k])
-            mine_a = out_probe.at[:, c, block(64, ia)]
-            gather_a[c, k] = remote(mine_a, mine_a, p_send.at[c, 3, k], p_recv.at[c, 3, k], peers_a[k])
+            scatter_b[c, k] = remote(part_b.at[c, :, block(16, jb)], got_b.at[c, k], *sems[1], peers_b[k])
+            mine_b = total.at[:, c, block(16, ib, ia * 64)]
+            gather_b[c, k] = remote(mine_b, mine_b, *sems[2], peers_b[k])
+            mine_a = total.at[:, c, block(64, ia)]
+            gather_a[c, k] = remote(mine_a, mine_a, *sems[3], peers_a[k])
         swap_y[c] = remote(y_send_buf.at[c], y_got.at[c], p_send.at[c, 4, 0], p_recv.at[c, 4, 0], y_peer)
+        probe_out[c] = pltpu.make_async_copy(total.at[:, c], out_probe.at[:, c], probe_sem.at[c])
+
+    def send_all(group, c):
+        for k in (1, 0, 2):
+            group[c, k].start()
+
+    def take_all(group, c):
+        for k in range(3):
+            group[c, k].wait_recv()
 
     def probe_1(c):
-        for k in (1, 0, 2):
-            scatter_a[c, k].start()
+        send_all(scatter_a, c)
 
     def probe_2(c):
         ia = axes[c][0][0]
-        for k in range(3):
-            scatter_a[c, k].wait_recv()
-        part_b[c] = partial[c, :, block(64, ia), :] + got_a[c, 0] + got_a[c, 1] + got_a[c, 2]
-        for k in (1, 0, 2):
-            scatter_b[c, k].start()
+        take_all(scatter_a, c)
+        got = got_a[c, 0] + got_a[c, 1] + got_a[c, 2]
+        part_b[c] = partial[c, :, block(64, ia), :] + got
+        send_all(scatter_b, c)
 
     def probe_3(c):
         ib = axes[c][1][0]
-        for k in range(3):
-            scatter_b[c, k].wait_recv()
-        y_send_buf[c] = part_b[c, :, block(16, ib), :] + got_b[c, 0] + got_b[c, 1] + got_b[c, 2]
+        take_all(scatter_b, c)
+        got = got_b[c, 0] + got_b[c, 1] + got_b[c, 2]
+        y_send_buf[c] = part_b[c, :, block(16, ib), :] + got
         swap_y[c].start()
 
     def probe_4(c):
         ia, ib = axes[c][0][0], axes[c][1][0]
         swap_y[c].wait_recv()
-        out_probe[:, c, block(16, ib, ia * 64), :] = y_send_buf[c] + y_got[c]
-        for k in (1, 0, 2):
-            gather_b[c, k].start()
+        total[:, c, block(16, ib, ia * 64), :] = y_send_buf[c] + y_got[c]
+        send_all(gather_b, c)
 
     def probe_5(c):
-        for k in range(3):
-            gather_b[c, k].wait_recv()
-        for k in (1, 0, 2):
-            gather_a[c, k].start()
+        take_all(gather_b, c)
+        send_all(gather_a, c)
 
     def probe_6(c):
-        for k in range(3):
-            gather_a[c, k].wait_recv()
+        take_all(gather_a, c)
+        probe_out[c].start()
+
+    def each(step):
+        for c in range(2):
+            step(c)
 
     to_share[0].wait_recv()
-    back_to_slice_1(0)
-    back_to_probe([(0, 0)])
+    over([(0, 0), (0, 1)], both_steps)
     factors(1)
     to_share[1].wait_recv()
-    back_to_slice_1(1)
-    reduce_start(1)
-    back_to_probe([(1, 0)])
+    over([(1, 0)], both_steps)
     probe_1(0)
-    back_to_probe([(0, 1), (1, 1)])
+    over([(1, 1)], both_steps)
     probe_1(1)
-    probe_2(0)
-    reduce_start(0)
-    probe_2(1)
-    probe_3(0)
-    reduce_middle(1)
-    probe_3(1)
-    probe_4(0)
-    reduce_middle(0)
-    probe_4(1)
-    probe_5(0)
-    reduce_end(1)
-    probe_5(1)
-    reduce_end(0)
-    probe_6(0)
-    probe_6(1)
-
+    reduce_1(1)
+    reduce_1(0)
+    reduce_2(1)
+    each(probe_2)
+    each(probe_3)
+    reduce_2(0)
+    each(probe_4)
+    reduce_3(1)
+    each(probe_5)
+    reduce_4(1)
+    reduce_3(0)
+    reduce_4(0)
+    each(probe_6)
+
+    for group in (probe_out, outward):
+        for copy in group.values():
+            copy.wait()
     for group in (scatter_a, scatter_b, swap_y, gather_b, gather_a):
         for copy in group.values():
             copy.wait_send()
@@ -532,12 +554,11 @@
     tiles = lax.axis_size("tile")
     shape = jax.ShapeDtypeStruct
     anywhere = pl.BlockSpec(memory_space=pl.ANY)
-    vmem = pl.BlockSpec(memory_space=pltpu.VMEM)
     return pl.pallas_call(
         functools.partial(kernel, tiles),
         out_shape=(shape(obj_re.shape, F32), shape(obj_im.shape, F32), shape(probe.shape, F32)),
         in_specs=[anywhere, anywhere, anywhere, anywhere, pl.BlockSpec(memory_space=pltpu.SMEM), anywhere, anywhere],
-        out_specs=(vmem, vmem, vmem),
+        out_specs=(anywhere, anywhere, anywhere),
         scratch_shapes=[
             pltpu.VMEM((2, TILE, TILE), F32),
             pltpu.VMEM((2, TILE, TILE), F32),
@@ -568,8 +589,8 @@
             pltpu.SemaphoreType.DMA((3, 2, 2)),
             pltpu.SemaphoreType.DMA((3, 2)),
             pltpu.SemaphoreType.DMA((3, 2)),
-            pltpu.SemaphoreType.DMA((3, 2)),
-            pltpu.SemaphoreType.DMA((3, 2)),
+            pltpu.SemaphoreType.DMA((5, 2)),
+            pltpu.SemaphoreType.DMA((5, 2)),
             pltpu.SemaphoreType.DMA((2, 2)),
             pltpu.SemaphoreType.DMA((2, 2)),
             pltpu.VMEM((2, 2, PX, PX), F32),
@@ -580,6 +601,9 @@
             pltpu.VMEM((2, 2, 16, PX), F32),
             pltpu.SemaphoreType.DMA((2, 5, 3)),
             pltpu.SemaphoreType.DMA((2, 5, 3)),
+            pltpu.VMEM((2, 2, PX, PX), F32),
+            pltpu.SemaphoreType.DMA((2, 2)),
+            pltpu.SemaphoreType.DMA((2,)),
         ],
         compiler_params=pltpu.CompilerParams(
             collective_id=0, has_side_effects=True, vmem_limit_bytes=56 * 1024 * 1024
@@ -588,9 +612,43 @@
     )(obj_re, obj_im, probe, measured, positions, table, orders)
 
 
+def deliver_kernel(count, *refs):
+    sources, targets, held = refs[:count], refs[count : 2 * count], refs[2 * count : 3 * count]
+    in_sem, out_sem = refs[3 * count :]
+    inward, outward = [], []
+    for i in range(count):
+        for k in range(2):
+            at = (slice(None), k)
+            inward.append(pltpu.make_async_copy(sources[i].at[at], held[i].at[at], in_sem.at[i, k]))
+            outward.append(pltpu.make_async_copy(held[i].at[at], targets[i].at[at], out_sem.at[i, k]))
+    for copy in inward:
+        copy.start()
+    for copy, onward in zip(inward, outward):
+        copy.wait()
+        onward.start()
+    for copy in outward:
+        copy.wait()
+
+
+def delivered(arrays):
+    anywhere = pl.BlockSpec(memory_space=pl.ANY)
+    count = len(arrays)
+    return pl.pallas_call(
+        functools.partial(deliver_kernel, count),
+        out_shape=tuple(jax.ShapeDtypeStruct(a.shape, a.dtype) for a in arrays),
+        in_specs=[anywhere] * count,
+        out_specs=(anywhere,) * count,
+        scratch_shapes=[pltpu.VMEM(a.shape, a.dtype) for a in arrays]
+        + [pltpu.SemaphoreType.DMA((count, 2)), pltpu.SemaphoreType.DMA((count, 2))],
+        compiler_params=pltpu.CompilerParams(vmem_limit_bytes=56 * 1024 * 1024),
+    )(*arrays)
+
+
 def body(object_real, object_imag, probe, measured, positions):
     table, orders = constants()
-    return gradients(object_real, object_imag, probe, measured, positions, jnp.asarray(table), jnp.asarray(orders))
+    return delivered(
+        gradients(object_real, object_imag, probe, measured, positions, jnp.asarray(table), jnp.asarray(orders))
+    )
 
 
 def solution(mesh):

time: 87.4 us -> 76.9 us (0.88)
  local copies, waits for them, and re-layouts: 5.67 us -> 0 us
  Pallas kernels: 80.7 us -> 76.2 us
    pallas_call x1, Pallas kernels: 80.7 us -> 73.7 us  [gradients(): pl.pallas_call(functools.partial(kernel, tiles), out_shape=(shape(obj_re....]
    unnamed x3 -> x0, local copies, waits for them, and re-layouts: 5.67 us -> none
    pallas_call x0 -> x1, Pallas kernels: none -> 2.41 us  [delivered(): pl.pallas_call(functools.partial(deliver_kernel, count), out_shape=tuple(...]
where the time goes in v2:
time: 76.9 us; the launch traced here: 76.8 us
  Pallas kernels  76.2 us (99%)
    pallas_call x1, Pallas kernels, gradients(): pl.pallas_call(functools.partial(kernel, tiles), out_shape=(shape(obj_re....  73.7 us
    pallas_call x1, Pallas kernels, delivered(): pl.pallas_call(functools.partial(deliver_kernel, count), out_shape=tuple(...  2.41 us

profile of v2, /device:TPU:0, one launch (start us, length us, event | category | flops | bytes accessed | tf_op | source)
XLA Modules:
  0.0 76.8 jit_solution(17500831335503486684)
XLA Ops:
  0.6 73.7 %shard_map.94 = (f32[1,2,96,384]{3,2,1,0:T(8,128)}, f32[1,2,96,384]{3,2,1,0:T(8,128)}, f32[2,2,256,256]{3,2,1,0:T(8,128)}) custom-call(f32[1,2,96,384]{3,2,1,0:T(8,128)} %obj_re.1, f32[1,2,96,384]{3,2,1,0:T(8,128)} %obj_im.1, f32[2,2,256,256]{3,2,1,0:T(8,128)} %probe_in.1, f32[1,2,256,256]{3,2,1,0:T(8,128)} %measured_in.1, s32[1,2,2]{2,1,0:T(2,128)} %positions.1, ...), custom_call_target="tpu_custom_call" | custom-call | flops 7000000000 | bytes 10000000 | tf_op jit(solution)/shard_map/pallas_call | solution.py:557
  74.4 2.4 %shard_map.95 = (f32[1,2,96,384]{3,2,1,0:T(8,128)}, f32[1,2,96,384]{3,2,1,0:T(8,128)}, f32[2,2,256,256]{3,2,1,0:T(8,128)}) custom-call(f32[1,2,96,384]{3,2,1,0:T(8,128)} %get-tuple-element.6.refs_0_, f32[1,2,96,384]{3,2,1,0:T(8,128)} %get-tuple-element.7.refs_1_, f32[2,2,256,256]{3,2,1,0:T(8,128)} %get-tuple-element.8.refs_2_), custom_call_target="tpu_custom_call" | custom-call | tf_op jit(solution)/shard_map/pallas_call | solution.py:636

commit v3 on v2

--- a/solution.py
+++ b/solution.py
@@ -261,8 +261,8 @@
     row = [positions[0, f, 0] for f in range(2)]
     col = [positions[0, f, 1] for f in range(2)]
 
-    def take_crops(s):
-        for f in range(2):
+    def take_crops(s, frames=(0, 1)):
+        for f in frames:
             up, back = lax.rem(TILE - row[f], TILE), lax.rem(TILE - col[f], TILE)
             for p in range(2):
                 lines = pltpu.roll(whole[s][p], up, 0)[:PX]
@@ -279,9 +279,9 @@
         wave1[f, mode, 1] = im
         return carry
 
-    lax.fori_loop(0, 4, pass_through, 0)
+    lax.fori_loop(0, 4, pass_through, 0, unroll=2)
     tile_ready(1)
-    take_crops(1)
+    take_crops(1, (0,))
 
     def far_fields(f):
         ipart[f] = jnp.zeros_like(ipart[f])
@@ -294,7 +294,7 @@
             ipart[f] += re * re + im * im
             return carry
 
-        lax.fori_loop(0, 2, step, 0)
+        lax.fori_loop(0, 2, step, 0, unroll=True)
 
     def half_rows(who):
         return pl.ds(pl.multiple_of(who * HALF, HALF), HALF)
@@ -327,6 +327,7 @@
 
     far_fields(0)
     to_pair[0].start()
+    take_crops(1, (1,))
     far_fields(1)
     to_pair[1].start()
     pair_sum(0)
@@ -368,26 +369,28 @@
         slice_1_step(f, mode)
         probe_step(f, mode)
 
-    def place(s):
-        for p in range(2):
-            placed = None
-            for f in range(2):
-                wide = jnp.concatenate([crop_grad[f, s, p], jnp.zeros((PX, EDGE), F32)], axis=1)
-                wide = pltpu.roll(wide, col[f], 1)
-                wide = jnp.concatenate([wide, jnp.zeros((EDGE, TILE), F32)], axis=0)
-                wide = pltpu.roll(wide, row[f], 0)
-                placed = wide if placed is None else placed + wide
-            tile_grad[s, p] = placed
+    low_lanes = lax.broadcasted_iota(jnp.int32, (TILE, 128), 1) < MARGIN
+
+    def place(s, f):
+        for p in range(2):
+            wide = jnp.concatenate([crop_grad[f, s, p], jnp.zeros((PX, EDGE), F32)], axis=1)
+            wide = pltpu.roll(wide, col[f], 1)
+            wide = jnp.concatenate([wide, jnp.zeros((EDGE, TILE), F32)], axis=0)
+            wide = pltpu.roll(wide, row[f], 0)
+            first, middle, last = wide[:, :128], wide[:, 128:256], wide[:, 256:]
+            ends, between = jnp.where(low_lanes, first, last), jnp.where(low_lanes, last, first)
+            blocks = jnp.concatenate([ends, middle, between], axis=1)
+            tile_grad[s, p] = blocks if f == 0 else tile_grad[s, p] + blocks
 
     def piece(s, p, who):
         return tile_grad[s, p, my_rows(who), :]
 
-    parts = (pl.ds(0, 128), pl.ds(TILE - 128, 128), pl.ds(128, TILE - 256))
+    parts = (pl.ds(0, 128), pl.ds(128, TILE - 128))
     rs_pair, rs_over, rs_edge, outward = {}, {}, {}, {}
     for s in range(2):
         for k in range(2):
             rs_pair[s, k] = remote(rs_send.at[s, k], rs_got.at[s, k], r_send.at[k, s], r_recv.at[k, s], to_sibling)
-        for k in range(3):
+        for k in range(2):
             rs_over[s, k] = remote(
                 rs_cross.at[s, :, :, parts[k]],
                 rs_cross_got.at[s, :, :, parts[k]],
@@ -401,7 +404,7 @@
             outward[s, p] = pltpu.make_async_copy(own.at[s, p], (out_re, out_im)[p].at[0, s], out_sem.at[s, p])
 
     def reduce_1(s):
-        place(s)
+        place(s, 1)
         for k, who in enumerate((diagonal, sibling)):
             for p in range(2):
                 rs_send[s, k, p] = piece(s, p, who)
@@ -411,8 +414,7 @@
         rs_pair[s, 0].wait_recv()
         for p in range(2):
             rs_cross[s, p] = piece(s, p, across) + rs_got[s, 0, p]
-        for k in range(3):
-            rs_over[s, k].start()
+        rs_over[s, 0].start()
         rs_pair[s, 1].wait_recv()
         for p in range(2):
             own[s, p] = piece(s, p, m) + rs_got[s, 1, p]
@@ -421,21 +423,16 @@
     lower = lane < MARGIN
 
     def reduce_3(s):
-        for k in range(2):
-            rs_over[s, k].wait_recv()
-            for p in range(2):
-                own[s, p, :, parts[k]] += rs_cross_got[s, p, :, parts[k]]
-        last = (own[s, 0, :, TILE - 128 :], own[s, 1, :, TILE - 128 :])
-        first = (own[s, 0, :, :128], own[s, 1, :, :128])
-        edge_send[s, 0] = jnp.where(lower, pltpu.roll(last[0], MARGIN, 1), last[1])
-        edge_send[s, 1] = jnp.where(lower, first[0], pltpu.roll(first[1], MARGIN, 1))
+        rs_over[s, 0].wait_recv()
+        ends = [own[s, p, :, :128] + rs_cross_got[s, p, :, :128] for p in range(2)]
+        for p in range(2):
+            own[s, p, :, :128] = ends[p]
+        edge_send[s, 0] = jnp.where(lower, pltpu.roll(ends[0], MARGIN, 1), ends[1])
+        edge_send[s, 1] = jnp.where(lower, ends[0], pltpu.roll(ends[1], MARGIN, 1))
         rs_edge[s, 0].start()
         rs_edge[s, 1].start()
 
     def reduce_4(s):
-        rs_over[s, 2].wait_recv()
-        for p in range(2):
-            own[s, p, :, parts[2]] += rs_cross_got[s, p, :, parts[2]]
         rs_edge[s, 0].wait_recv()
         rs_edge[s, 1].wait_recv()
         before, after = edge_got[s, 0], edge_got[s, 1]
@@ -443,9 +440,13 @@
         at_last = jnp.logical_and(jnp.logical_not(lower), t < tiles - 1)
         befores = (before, pltpu.roll(before, MARGIN, 1))
         afters = (pltpu.roll(after, MARGIN, 1), after)
-        for p in range(2):
-            own[s, p, :, parts[0]] += jnp.where(at_first, befores[p], 0.0)
-            own[s, p, :, parts[1]] += jnp.where(at_last, afters[p], 0.0)
+        rs_over[s, 1].wait_recv()
+        for p in range(2):
+            ends = own[s, p, :, :128] + jnp.where(at_first, befores[p], 0.0) + jnp.where(at_last, afters[p], 0.0)
+            between = own[s, p, :, 256:] + rs_cross_got[s, p, :, 256:]
+            own[s, p, :, 128:256] += rs_cross_got[s, p, :, 128:256]
+            own[s, p, :, :128] = jnp.where(lower, ends, between)
+            own[s, p, :, 256:] = jnp.where(lower, between, ends)
             outward[s, p].start()
 
     axes = (((tz, z_peers), (tx, x_peers)), ((tx, x_peers), (tz, z_peers)))
@@ -454,69 +455,74 @@
         return pl.ds(pl.multiple_of(base + index * length, length), length)
 
     scatter_a, scatter_b, swap_y, gather_b, gather_a, probe_out = {}, {}, {}, {}, {}, {}
-    chunks = range(2)
-    for c in chunks:
+    chunks = [(c, h) for h in range(2) for c in range(2)]
+    for c, h in chunks:
         (ia, peers_a), (ib, peers_b) = axes[c]
         for k in range(ring - 1):
             ja, jb = lax.rem(ia + k + 1, ring), lax.rem(ib + k + 1, ring)
-            sems = [(p_send.at[c, i, k], p_recv.at[c, i, k]) for i in range(4)]
-            scatter_a[c, k] = remote(
-                partial.at[c, :, block(64, ja)], got_a.at[c, k], *sems[0], peers_a[k]
+            sems = [(p_send.at[c, h, i, k], p_recv.at[c, h, i, k]) for i in range(4)]
+            scatter_a[c, h, k] = remote(
+                partial.at[c, :, block(32, ja, h * HALF)], got_a.at[c, h, k], *sems[0], peers_a[k]
             )
-            scatter_b[c, k] = remote(part_b.at[c, :, block(16, jb)], got_b.at[c, k], *sems[1], peers_b[k])
-            mine_b = total.at[:, c, block(16, ib, ia * 64)]
-            gather_b[c, k] = remote(mine_b, mine_b, *sems[2], peers_b[k])
-            mine_a = total.at[:, c, block(64, ia)]
-            gather_a[c, k] = remote(mine_a, mine_a, *sems[3], peers_a[k])
-        swap_y[c] = remote(y_send_buf.at[c], y_got.at[c], p_send.at[c, 4, 0], p_recv.at[c, 4, 0], y_peer)
-        probe_out[c] = pltpu.make_async_copy(total.at[:, c], out_probe.at[:, c], probe_sem.at[c])
-
-    def send_all(group, c):
+            scatter_b[c, h, k] = remote(part_b.at[c, h, :, block(8, jb)], got_b.at[c, h, k], *sems[1], peers_b[k])
+            mine_b = total.at[:, c, block(8, ib, h * HALF + ia * 32)]
+            gather_b[c, h, k] = remote(mine_b, mine_b, *sems[2], peers_b[k])
+            mine_a = total.at[:, c, block(32, ia, h * HALF)]
+            gather_a[c, h, k] = remote(mine_a, mine_a, *sems[3], peers_a[k])
+        swap_y[c, h] = remote(y_send_buf.at[c, h], y_got.at[c, h], p_send.at[c, h, 4, 0], p_recv.at[c, h, 4, 0], y_peer)
+        some = pl.ds(h * HALF, HALF)
+        probe_out[c, h] = pltpu.make_async_copy(total.at[:, c, some], out_probe.at[:, c, some], probe_sem.at[c, h])
+
+    def send_all(group, c, h):
         for k in (1, 0, 2):
-            group[c, k].start()
-
-    def take_all(group, c):
+            group[c, h, k].start()
+
+    def take_all(group, c, h):
         for k in range(3):
-            group[c, k].wait_recv()
+            group[c, h, k].wait_recv()
 
     def probe_1(c):
-        send_all(scatter_a, c)
-
-    def probe_2(c):
+        for h in range(2):
+            send_all(scatter_a, c, h)
+
+    def probe_2(c, h):
         ia = axes[c][0][0]
-        take_all(scatter_a, c)
-        got = got_a[c, 0] + got_a[c, 1] + got_a[c, 2]
-        part_b[c] = partial[c, :, block(64, ia), :] + got
-        send_all(scatter_b, c)
-
-    def probe_3(c):
+        take_all(scatter_a, c, h)
+        got = got_a[c, h, 0] + got_a[c, h, 1] + got_a[c, h, 2]
+        part_b[c, h] = partial[c, :, block(32, ia, h * HALF), :] + got
+        send_all(scatter_b, c, h)
+
+    def probe_3(c, h):
         ib = axes[c][1][0]
-        take_all(scatter_b, c)
-        got = got_b[c, 0] + got_b[c, 1] + got_b[c, 2]
-        y_send_buf[c] = part_b[c, :, block(16, ib), :] + got
-        swap_y[c].start()
-
-    def probe_4(c):
+        take_all(scatter_b, c, h)
+        got = got_b[c, h, 0] + got_b[c, h, 1] + got_b[c, h, 2]
+        y_send_buf[c, h] = part_b[c, h, :, block(8, ib), :] + got
+        swap_y[c, h].start()
+
+    def probe_4(c, h):
         ia, ib = axes[c][0][0], axes[c][1][0]
-        swap_y[c].wait_recv()
-        total[:, c, block(16, ib, ia * 64), :] = y_send_buf[c] + y_got[c]
-        send_all(gather_b, c)
-
-    def probe_5(c):
-        take_all(gather_b, c)
-        send_all(gather_a, c)
-
-    def probe_6(c):
-        take_all(gather_a, c)
-        probe_out[c].start()
-
-    def each(step):
+        swap_y[c, h].wait_recv()
+        total[:, c, block(8, ib, h * HALF + ia * 32), :] = y_send_buf[c, h] + y_got[c, h]
+        send_all(gather_b, c, h)
+
+    def probe_5(c, h):
+        take_all(gather_b, c, h)
+        send_all(gather_a, c, h)
+
+    def probe_6(c, h):
+        take_all(gather_a, c, h)
+        probe_out[c, h].start()
+
+    def each(step, h):
         for c in range(2):
-            step(c)
+            step(c, h)
 
     to_share[0].wait_recv()
-    over([(0, 0), (0, 1)], both_steps)
+    over([(0, 0)], both_steps)
     factors(1)
+    over([(0, 1)], both_steps)
+    place(1, 0)
+    place(0, 0)
     to_share[1].wait_recv()
     over([(1, 0)], both_steps)
     probe_1(0)
@@ -525,16 +531,23 @@
     reduce_1(1)
     reduce_1(0)
     reduce_2(1)
-    each(probe_2)
-    each(probe_3)
     reduce_2(0)
-    each(probe_4)
+    each(probe_2, 0)
+    each(probe_2, 1)
+    each(probe_3, 0)
     reduce_3(1)
-    each(probe_5)
+    each(probe_3, 1)
+    rs_over[1, 1].start()
+    rs_over[0, 1].start()
+    each(probe_4, 0)
+    reduce_3(0)
+    each(probe_4, 1)
+    each(probe_5, 0)
+    each(probe_5, 1)
     reduce_4(1)
-    reduce_3(0)
+    each(probe_6, 0)
     reduce_4(0)
-    each(probe_6)
+    each(probe_6, 1)
 
     for group in (probe_out, outward):
         for copy in group.values():
@@ -594,16 +607,16 @@
             pltpu.SemaphoreType.DMA((2, 2)),
             pltpu.SemaphoreType.DMA((2, 2)),
             pltpu.VMEM((2, 2, PX, PX), F32),
-            pltpu.VMEM((2, 3, 2, 64, PX), F32),
-            pltpu.VMEM((2, 3, 2, 16, PX), F32),
-            pltpu.VMEM((2, 2, 64, PX), F32),
-            pltpu.VMEM((2, 2, 16, PX), F32),
-            pltpu.VMEM((2, 2, 16, PX), F32),
-            pltpu.SemaphoreType.DMA((2, 5, 3)),
-            pltpu.SemaphoreType.DMA((2, 5, 3)),
+            pltpu.VMEM((2, 2, 3, 2, 32, PX), F32),
+            pltpu.VMEM((2, 2, 3, 2, 8, PX), F32),
+            pltpu.VMEM((2, 2, 2, 32, PX), F32),
+            pltpu.VMEM((2, 2, 2, 8, PX), F32),
+            pltpu.VMEM((2, 2, 2, 8, PX), F32),
+            pltpu.SemaphoreType.DMA((2, 2, 5, 3)),
+            pltpu.SemaphoreType.DMA((2, 2, 5, 3)),
             pltpu.VMEM((2, 2, PX, PX), F32),
             pltpu.SemaphoreType.DMA((2, 2)),
-            pltpu.SemaphoreType.DMA((2,)),
+            pltpu.SemaphoreType.DMA((2, 2)),
         ],
         compiler_params=pltpu.CompilerParams(
             collective_id=0, has_side_effects=True, vmem_limit_bytes=56 * 1024 * 1024

time: 76.9 us -> 72 us (0.936)
  Pallas kernels: 76.2 us -> 70.8 us
    pallas_call x1, Pallas kernels: 73.7 us -> 68.4 us  [gradients(): pl.pallas_call(functools.partial(kernel, tiles), out_shape=(shape(obj_re....]
where the time goes in v3:
time: 72 us; the launch traced here: 71.6 us
  Pallas kernels  70.8 us (98%)
  between operations  0.8 us (1%)
    pallas_call x1, Pallas kernels, gradients(): pl.pallas_call(functools.partial(kernel, tiles), out_shape=(shape(obj_re....  68.4 us
    pallas_call x1, Pallas kernels, delivered(): pl.pallas_call(functools.partial(deliver_kernel, count), out_shape=tuple(...  2.41 us

profile of v3, /device:TPU:0, one launch (start us, length us, event | category | flops | bytes accessed | tf_op | source)
XLA Modules:
  0.0 71.6 jit_solution(16967537975637486589)
XLA Ops:
  0.6 68.4 %shard_map.94 = (f32[1,2,96,384]{3,2,1,0:T(8,128)}, f32[1,2,96,384]{3,2,1,0:T(8,128)}, f32[2,2,256,256]{3,2,1,0:T(8,128)}) custom-call(f32[1,2,96,384]{3,2,1,0:T(8,128)} %obj_re.1, f32[1,2,96,384]{3,2,1,0:T(8,128)} %obj_im.1, f32[2,2,256,256]{3,2,1,0:T(8,128)} %probe_in.1, f32[1,2,256,256]{3,2,1,0:T(8,128)} %measured_in.1, s32[1,2,2]{2,1,0:T(2,128)} %positions.1, ...), custom_call_target="tpu_custom_call" | custom-call | flops 7000000000 | bytes 10000000 | tf_op jit(solution)/shard_map/pallas_call | solution.py:570
  69.0 2.4 %shard_map.95 = (f32[1,2,96,384]{3,2,1,0:T(8,128)}, f32[1,2,96,384]{3,2,1,0:T(8,128)}, f32[2,2,256,256]{3,2,1,0:T(8,128)}) custom-call(f32[1,2,96,384]{3,2,1,0:T(8,128)} %get-tuple-element.6.refs_0_, f32[1,2,96,384]{3,2,1,0:T(8,128)} %get-tuple-element.7.refs_1_, f32[2,2,256,256]{3,2,1,0:T(8,128)} %get-tuple-element.8.refs_2_), custom_call_target="tpu_custom_call" | custom-call | tf_op jit(solution)/shard_map/pallas_call | solution.py:649

commit v4 on v3

--- a/solution.py
+++ b/solution.py
@@ -147,7 +147,6 @@
     factor,
     crop_grad,
     tile_grad,
-    rs_send,
     rs_got,
     rs_cross,
     rs_cross_got,
@@ -388,8 +387,9 @@
     parts = (pl.ds(0, 128), pl.ds(128, TILE - 128))
     rs_pair, rs_over, rs_edge, outward = {}, {}, {}, {}
     for s in range(2):
-        for k in range(2):
-            rs_pair[s, k] = remote(rs_send.at[s, k], rs_got.at[s, k], r_send.at[k, s], r_recv.at[k, s], to_sibling)
+        for k, who in enumerate((diagonal, sibling)):
+            lines = tile_grad.at[s, :, my_rows(who)]
+            rs_pair[s, k] = remote(lines, rs_got.at[s, k], r_send.at[k, s], r_recv.at[k, s], to_sibling)
         for k in range(2):
             rs_over[s, k] = remote(
                 rs_cross.at[s, :, :, parts[k]],
@@ -405,9 +405,7 @@
 
     def reduce_1(s):
         place(s, 1)
-        for k, who in enumerate((diagonal, sibling)):
-            for p in range(2):
-                rs_send[s, k, p] = piece(s, p, who)
+        for k in range(2):
             rs_pair[s, k].start()
 
     def reduce_2(s):
@@ -415,6 +413,8 @@
         for p in range(2):
             rs_cross[s, p] = piece(s, p, across) + rs_got[s, 0, p]
         rs_over[s, 0].start()
+
+    def reduce_own(s):
         rs_pair[s, 1].wait_recv()
         for p in range(2):
             own[s, p] = piece(s, p, m) + rs_got[s, 1, p]
@@ -534,7 +534,9 @@
     reduce_2(0)
     each(probe_2, 0)
     each(probe_2, 1)
+    reduce_own(1)
     each(probe_3, 0)
+    reduce_own(0)
     reduce_3(1)
     each(probe_3, 1)
     rs_over[1, 1].start()
@@ -589,7 +591,6 @@
             pltpu.VMEM((2, PX, PX), F32),
             pltpu.VMEM((2, 2, 2, PX, PX), F32),
             pltpu.VMEM((2, 2, TILE, TILE), F32),
-            pltpu.VMEM((2, 2, 2, ROWS, TILE), F32),
             pltpu.VMEM((2, 2, 2, ROWS, TILE), F32),
             pltpu.VMEM((2, 2, ROWS, TILE), F32),
             pltpu.VMEM((2, 2, ROWS, TILE), F32),

time: 72 us -> 72.1 us (level)
  no operation moved by 1% of the time
where the time goes in v4:
time: 72.1 us; the launch traced here: 71.5 us
  Pallas kernels  70.7 us (98%)
  between operations  0.8 us (1%)
    pallas_call x1, Pallas kernels, gradients(): pl.pallas_call(functools.partial(kernel, tiles), out_shape=(shape(obj_re....  68.3 us
    pallas_call x1, Pallas kernels, delivered(): pl.pallas_call(functools.partial(deliver_kernel, count), out_shape=tuple(...  2.41 us

profile of v4, /device:TPU:0, one launch (start us, length us, event | category | flops | bytes accessed | tf_op | source)
XLA Modules:
  0.0 71.5 jit_solution(8941915155539287838)
XLA Ops:
  0.6 68.3 %shard_map.94 = (f32[1,2,96,384]{3,2,1,0:T(8,128)}, f32[1,2,96,384]{3,2,1,0:T(8,128)}, f32[2,2,256,256]{3,2,1,0:T(8,128)}) custom-call(f32[1,2,96,384]{3,2,1,0:T(8,128)} %obj_re.1, f32[1,2,96,384]{3,2,1,0:T(8,128)} %obj_im.1, f32[2,2,256,256]{3,2,1,0:T(8,128)} %probe_in.1, f32[1,2,256,256]{3,2,1,0:T(8,128)} %measured_in.1, s32[1,2,2]{2,1,0:T(2,128)} %positions.1, ...), custom_call_target="tpu_custom_call" | custom-call | flops 7000000000 | bytes 10000000 | tf_op jit(solution)/shard_map/pallas_call | solution.py:572
  68.9 2.4 %shard_map.95 = (f32[1,2,96,384]{3,2,1,0:T(8,128)}, f32[1,2,96,384]{3,2,1,0:T(8,128)}, f32[2,2,256,256]{3,2,1,0:T(8,128)}) custom-call(f32[1,2,96,384]{3,2,1,0:T(8,128)} %get-tuple-element.6.refs_0_, f32[1,2,96,384]{3,2,1,0:T(8,128)} %get-tuple-element.7.refs_1_, f32[2,2,256,256]{3,2,1,0:T(8,128)} %get-tuple-element.8.refs_2_), custom_call_target="tpu_custom_call" | custom-call | tf_op jit(solution)/shard_map/pallas_call | solution.py:650

commit v5 on v3

--- a/solution.py
+++ b/solution.py
@@ -630,8 +630,9 @@
     in_sem, out_sem = refs[3 * count :]
     inward, outward = [], []
     for i in range(count):
-        for k in range(2):
-            at = (slice(None), k)
+        rows = sources[i].shape[2] // 2
+        for k in range(4):
+            at = (slice(None), k // 2, pl.ds(k % 2 * rows, rows))
             inward.append(pltpu.make_async_copy(sources[i].at[at], held[i].at[at], in_sem.at[i, k]))
             outward.append(pltpu.make_async_copy(held[i].at[at], targets[i].at[at], out_sem.at[i, k]))
     for copy in inward:
@@ -652,7 +653,7 @@
         in_specs=[anywhere] * count,
         out_specs=(anywhere,) * count,
         scratch_shapes=[pltpu.VMEM(a.shape, a.dtype) for a in arrays]
-        + [pltpu.SemaphoreType.DMA((count, 2)), pltpu.SemaphoreType.DMA((count, 2))],
+        + [pltpu.SemaphoreType.DMA((count, 4)), pltpu.SemaphoreType.DMA((count, 4))],
         compiler_params=pltpu.CompilerParams(vmem_limit_bytes=56 * 1024 * 1024),
     )(*arrays)
 

time: 72 us -> 72 us (level)
  no operation moved by 1% of the time
where the time goes in v5:
time: 72 us; the launch traced here: 71.6 us
  Pallas kernels  70.8 us (98%)
  between operations  0.8 us (1%)
    pallas_call x1, Pallas kernels, gradients(): pl.pallas_call(functools.partial(kernel, tiles), out_shape=(shape(obj_re....  68.4 us
    pallas_call x1, Pallas kernels, delivered(): pl.pallas_call(functools.partial(deliver_kernel, count), out_shape=tuple(...  2.41 us

profile of v5, /device:TPU:0, one launch (start us, length us, event | category | flops | bytes accessed | tf_op | source)
XLA Modules:
  0.0 71.6 jit_solution(13173155424035902881)
XLA Ops:
  0.6 68.4 %shard_map.94 = (f32[1,2,96,384]{3,2,1,0:T(8,128)}, f32[1,2,96,384]{3,2,1,0:T(8,128)}, f32[2,2,256,256]{3,2,1,0:T(8,128)}) custom-call(f32[1,2,96,384]{3,2,1,0:T(8,128)} %obj_re.1, f32[1,2,96,384]{3,2,1,0:T(8,128)} %obj_im.1, f32[2,2,256,256]{3,2,1,0:T(8,128)} %probe_in.1, f32[1,2,256,256]{3,2,1,0:T(8,128)} %measured_in.1, s32[1,2,2]{2,1,0:T(2,128)} %positions.1, ...), custom_call_target="tpu_custom_call" | custom-call | flops 7000000000 | bytes 10000000 | tf_op jit(solution)/shard_map/pallas_call | solution.py:570
  69.0 2.4 %shard_map.95 = (f32[1,2,96,384]{3,2,1,0:T(8,128)}, f32[1,2,96,384]{3,2,1,0:T(8,128)}, f32[2,2,256,256]{3,2,1,0:T(8,128)}) custom-call(f32[1,2,96,384]{3,2,1,0:T(8,128)} %get-tuple-element.6.refs_0_, f32[1,2,96,384]{3,2,1,0:T(8,128)} %get-tuple-element.7.refs_1_, f32[2,2,256,256]{3,2,1,0:T(8,128)} %get-tuple-element.8.refs_2_), custom_call_target="tpu_custom_call" | custom-call | tf_op jit(solution)/shard_map/pallas_call | solution.py:650

commit v6 on v3

--- a/solution.py
+++ b/solution.py
@@ -455,23 +455,27 @@
         return pl.ds(pl.multiple_of(base + index * length, length), length)
 
     scatter_a, scatter_b, swap_y, gather_b, gather_a, probe_out = {}, {}, {}, {}, {}, {}
-    chunks = [(c, h) for h in range(2) for c in range(2)]
+    chunks = [(c, h) for h in range(4) for c in range(2)]
+
+    def quarter(h, length, index, base=0):
+        return block(length, index, h // 2 * HALF + base), pl.ds(h % 2 * HALF, HALF)
+
     for c, h in chunks:
         (ia, peers_a), (ib, peers_b) = axes[c]
         for k in range(ring - 1):
             ja, jb = lax.rem(ia + k + 1, ring), lax.rem(ib + k + 1, ring)
             sems = [(p_send.at[c, h, i, k], p_recv.at[c, h, i, k]) for i in range(4)]
             scatter_a[c, h, k] = remote(
-                partial.at[c, :, block(32, ja, h * HALF)], got_a.at[c, h, k], *sems[0], peers_a[k]
+                partial.at[(c, slice(None), *quarter(h, 32, ja))], got_a.at[c, h, k], *sems[0], peers_a[k]
             )
             scatter_b[c, h, k] = remote(part_b.at[c, h, :, block(8, jb)], got_b.at[c, h, k], *sems[1], peers_b[k])
-            mine_b = total.at[:, c, block(8, ib, h * HALF + ia * 32)]
+            mine_b = total.at[(slice(None), c, *quarter(h, 8, ib, ia * 32))]
             gather_b[c, h, k] = remote(mine_b, mine_b, *sems[2], peers_b[k])
-            mine_a = total.at[:, c, block(32, ia, h * HALF)]
+            mine_a = total.at[(slice(None), c, *quarter(h, 32, ia))]
             gather_a[c, h, k] = remote(mine_a, mine_a, *sems[3], peers_a[k])
         swap_y[c, h] = remote(y_send_buf.at[c, h], y_got.at[c, h], p_send.at[c, h, 4, 0], p_recv.at[c, h, 4, 0], y_peer)
-        some = pl.ds(h * HALF, HALF)
-        probe_out[c, h] = pltpu.make_async_copy(total.at[:, c, some], out_probe.at[:, c, some], probe_sem.at[c, h])
+        some = (slice(None), c, pl.ds(h // 2 * HALF, HALF), pl.ds(h % 2 * HALF, HALF))
+        probe_out[c, h] = pltpu.make_async_copy(total.at[some], out_probe.at[some], probe_sem.at[c, h])
 
     def send_all(group, c, h):
         for k in (1, 0, 2):
@@ -482,14 +486,14 @@
             group[c, h, k].wait_recv()
 
     def probe_1(c):
-        for h in range(2):
+        for h in range(4):
             send_all(scatter_a, c, h)
 
     def probe_2(c, h):
         ia = axes[c][0][0]
         take_all(scatter_a, c, h)
         got = got_a[c, h, 0] + got_a[c, h, 1] + got_a[c, h, 2]
-        part_b[c, h] = partial[c, :, block(32, ia, h * HALF), :] + got
+        part_b[c, h] = partial[(c, slice(None), *quarter(h, 32, ia))] + got
         send_all(scatter_b, c, h)
 
     def probe_3(c, h):
@@ -502,7 +506,7 @@
     def probe_4(c, h):
         ia, ib = axes[c][0][0], axes[c][1][0]
         swap_y[c, h].wait_recv()
-        total[:, c, block(8, ib, h * HALF + ia * 32), :] = y_send_buf[c, h] + y_got[c, h]
+        total[(slice(None), c, *quarter(h, 8, ib, ia * 32))] = y_send_buf[c, h] + y_got[c, h]
         send_all(gather_b, c, h)
 
     def probe_5(c, h):
@@ -535,19 +539,29 @@
     each(probe_2, 0)
     each(probe_2, 1)
     each(probe_3, 0)
+    each(probe_2, 2)
+    each(probe_3, 1)
+    each(probe_2, 3)
+    each(probe_3, 2)
+    each(probe_4, 0)
     reduce_3(1)
-    each(probe_3, 1)
+    each(probe_3, 3)
     rs_over[1, 1].start()
     rs_over[0, 1].start()
-    each(probe_4, 0)
+    each(probe_4, 1)
     reduce_3(0)
-    each(probe_4, 1)
     each(probe_5, 0)
+    each(probe_4, 2)
     each(probe_5, 1)
+    each(probe_4, 3)
+    each(probe_5, 2)
+    each(probe_5, 3)
     reduce_4(1)
     each(probe_6, 0)
+    each(probe_6, 1)
+    each(probe_6, 2)
     reduce_4(0)
-    each(probe_6, 1)
+    each(probe_6, 3)
 
     for group in (probe_out, outward):
         for copy in group.values():
@@ -607,16 +621,16 @@
             pltpu.SemaphoreType.DMA((2, 2)),
             pltpu.SemaphoreType.DMA((2, 2)),
             pltpu.VMEM((2, 2, PX, PX), F32),
-            pltpu.VMEM((2, 2, 3, 2, 32, PX), F32),
-            pltpu.VMEM((2, 2, 3, 2, 8, PX), F32),
-            pltpu.VMEM((2, 2, 2, 32, PX), F32),
-            pltpu.VMEM((2, 2, 2, 8, PX), F32),
-            pltpu.VMEM((2, 2, 2, 8, PX), F32),
-            pltpu.SemaphoreType.DMA((2, 2, 5, 3)),
-            pltpu.SemaphoreType.DMA((2, 2, 5, 3)),
+            pltpu.VMEM((2, 4, 3, 2, 32, HALF), F32),
+            pltpu.VMEM((2, 4, 3, 2, 8, HALF), F32),
+            pltpu.VMEM((2, 4, 2, 32, HALF), F32),
+            pltpu.VMEM((2, 4, 2, 8, HALF), F32),
+            pltpu.VMEM((2, 4, 2, 8, HALF), F32),
+            pltpu.SemaphoreType.DMA((2, 4, 5, 3)),
+            pltpu.SemaphoreType.DMA((2, 4, 5, 3)),
             pltpu.VMEM((2, 2, PX, PX), F32),
             pltpu.SemaphoreType.DMA((2, 2)),
-            pltpu.SemaphoreType.DMA((2, 2)),
+            pltpu.SemaphoreType.DMA((2, 4)),
         ],
         compiler_params=pltpu.CompilerParams(
             collective_id=0, has_side_effects=True, vmem_limit_bytes=56 * 1024 * 1024

time: 72 us -> 75.4 us (1.047)
  Pallas kernels: 70.8 us -> 74.3 us
    pallas_call x1, Pallas kernels: 68.4 us -> 71.9 us  [gradients(): pl.pallas_call(functools.partial(kernel, tiles), out_shape=(shape(obj_re....]
where the time goes in v6:
time: 75.4 us; the launch traced here: 75.1 us
  Pallas kernels  74.3 us (99%)
  between operations  0.8 us (1%)
    pallas_call x1, Pallas kernels, gradients(): pl.pallas_call(functools.partial(kernel, tiles), out_shape=(shape(obj_re....  71.9 us
    pallas_call x1, Pallas kernels, delivered(): pl.pallas_call(functools.partial(deliver_kernel, count), out_shape=tuple(...  2.41 us

profile of v6, /device:TPU:0, one launch (start us, length us, event | category | flops | bytes accessed | tf_op | source)
XLA Modules:
  0.0 75.1 jit_solution(15346422402070554705)
XLA Ops:
  0.6 71.9 %shard_map.94 = (f32[1,2,96,384]{3,2,1,0:T(8,128)}, f32[1,2,96,384]{3,2,1,0:T(8,128)}, f32[2,2,256,256]{3,2,1,0:T(8,128)}) custom-call(f32[1,2,96,384]{3,2,1,0:T(8,128)} %obj_re.1, f32[1,2,96,384]{3,2,1,0:T(8,128)} %obj_im.1, f32[2,2,256,256]{3,2,1,0:T(8,128)} %probe_in.1, f32[1,2,256,256]{3,2,1,0:T(8,128)} %measured_in.1, s32[1,2,2]{2,1,0:T(2,128)} %positions.1, ...), custom_call_target="tpu_custom_call" | custom-call | flops 7000000000 | bytes 10000000 | tf_op jit(solution)/shard_map/pallas_call | solution.py:584
  72.5 2.4 %shard_map.95 = (f32[1,2,96,384]{3,2,1,0:T(8,128)}, f32[1,2,96,384]{3,2,1,0:T(8,128)}, f32[2,2,256,256]{3,2,1,0:T(8,128)}) custom-call(f32[1,2,96,384]{3,2,1,0:T(8,128)} %get-tuple-element.6.refs_0_, f32[1,2,96,384]{3,2,1,0:T(8,128)} %get-tuple-element.7.refs_1_, f32[2,2,256,256]{3,2,1,0:T(8,128)} %get-tuple-element.8.refs_2_), custom_call_target="tpu_custom_call" | custom-call | tf_op jit(solution)/shard_map/pallas_call | solution.py:663

commit v7 on v3

--- a/solution.py
+++ b/solution.py
@@ -414,7 +414,8 @@
         rs_pair[s, 0].wait_recv()
         for p in range(2):
             rs_cross[s, p] = piece(s, p, across) + rs_got[s, 0, p]
-        rs_over[s, 0].start()
+        if s == 1:
+            rs_over[s, 0].start()
         rs_pair[s, 1].wait_recv()
         for p in range(2):
             own[s, p] = piece(s, p, m) + rs_got[s, 1, p]
@@ -535,6 +536,7 @@
     each(probe_2, 0)
     each(probe_2, 1)
     each(probe_3, 0)
+    rs_over[0, 0].start()
     reduce_3(1)
     each(probe_3, 1)
     rs_over[1, 1].start()

time: 72 us -> 73.9 us (1.026)
  Pallas kernels: 70.8 us -> 73 us
    pallas_call x1, Pallas kernels: 68.4 us -> 70.6 us  [gradients(): pl.pallas_call(functools.partial(kernel, tiles), out_shape=(shape(obj_re....]
where the time goes in v7:
time: 73.9 us; the launch traced here: 73.8 us
  Pallas kernels  73 us (99%)
  between operations  0.8 us (1%)
    pallas_call x1, Pallas kernels, gradients(): pl.pallas_call(functools.partial(kernel, tiles), out_shape=(shape(obj_re....  70.6 us
    pallas_call x1, Pallas kernels, delivered(): pl.pallas_call(functools.partial(deliver_kernel, count), out_shape=tuple(...  2.41 us

profile of v7, /device:TPU:0, one launch (start us, length us, event | category | flops | bytes accessed | tf_op | source)
XLA Modules:
  0.0 73.8 jit_solution(15160894839013682552)
XLA Ops:
  0.6 70.6 %shard_map.94 = (f32[1,2,96,384]{3,2,1,0:T(8,128)}, f32[1,2,96,384]{3,2,1,0:T(8,128)}, f32[2,2,256,256]{3,2,1,0:T(8,128)}) custom-call(f32[1,2,96,384]{3,2,1,0:T(8,128)} %obj_re.1, f32[1,2,96,384]{3,2,1,0:T(8,128)} %obj_im.1, f32[2,2,256,256]{3,2,1,0:T(8,128)} %probe_in.1, f32[1,2,256,256]{3,2,1,0:T(8,128)} %measured_in.1, s32[1,2,2]{2,1,0:T(2,128)} %positions.1, ...), custom_call_target="tpu_custom_call" | custom-call | flops 7000000000 | bytes 10000000 | tf_op jit(solution)/shard_map/pallas_call | solution.py:572
  71.2 2.4 %shard_map.95 = (f32[1,2,96,384]{3,2,1,0:T(8,128)}, f32[1,2,96,384]{3,2,1,0:T(8,128)}, f32[2,2,256,256]{3,2,1,0:T(8,128)}) custom-call(f32[1,2,96,384]{3,2,1,0:T(8,128)} %get-tuple-element.6.refs_0_, f32[1,2,96,384]{3,2,1,0:T(8,128)} %get-tuple-element.7.refs_1_, f32[2,2,256,256]{3,2,1,0:T(8,128)} %get-tuple-element.8.refs_2_), custom_call_target="tpu_custom_call" | custom-call | tf_op jit(solution)/shard_map/pallas_call | solution.py:651

commit v8 on v3

--- a/solution.py
+++ b/solution.py
@@ -537,10 +537,10 @@
     each(probe_3, 0)
     reduce_3(1)
     each(probe_3, 1)
+    reduce_3(0)
     rs_over[1, 1].start()
     rs_over[0, 1].start()
     each(probe_4, 0)
-    reduce_3(0)
     each(probe_4, 1)
     each(probe_5, 0)
     each(probe_5, 1)

time: 72 us -> 71.8 us (level)
  no operation moved by 1% of the time
where the time goes in v8:
time: 71.8 us; the launch traced here: 71.2 us
  Pallas kernels  70.4 us (98%)
  between operations  0.8 us (1%)
    pallas_call x1, Pallas kernels, gradients(): pl.pallas_call(functools.partial(kernel, tiles), out_shape=(shape(obj_re....  68 us
    pallas_call x1, Pallas kernels, delivered(): pl.pallas_call(functools.partial(deliver_kernel, count), out_shape=tuple(...  2.41 us

profile of v8, /device:TPU:0, one launch (start us, length us, event | category | flops | bytes accessed | tf_op | source)
XLA Modules:
  0.0 71.2 jit_solution(5469889682538726781)
XLA Ops:
  0.6 68.0 %shard_map.94 = (f32[1,2,96,384]{3,2,1,0:T(8,128)}, f32[1,2,96,384]{3,2,1,0:T(8,128)}, f32[2,2,256,256]{3,2,1,0:T(8,128)}) custom-call(f32[1,2,96,384]{3,2,1,0:T(8,128)} %obj_re.1, f32[1,2,96,384]{3,2,1,0:T(8,128)} %obj_im.1, f32[2,2,256,256]{3,2,1,0:T(8,128)} %probe_in.1, f32[1,2,256,256]{3,2,1,0:T(8,128)} %measured_in.1, s32[1,2,2]{2,1,0:T(2,128)} %positions.1, ...), custom_call_target="tpu_custom_call" | custom-call | flops 7000000000 | bytes 10000000 | tf_op jit(solution)/shard_map/pallas_call | solution.py:570
  68.6 2.4 %shard_map.95 = (f32[1,2,96,384]{3,2,1,0:T(8,128)}, f32[1,2,96,384]{3,2,1,0:T(8,128)}, f32[2,2,256,256]{3,2,1,0:T(8,128)}) custom-call(f32[1,2,96,384]{3,2,1,0:T(8,128)} %get-tuple-element.6.refs_0_, f32[1,2,96,384]{3,2,1,0:T(8,128)} %get-tuple-element.7.refs_1_, f32[2,2,256,256]{3,2,1,0:T(8,128)} %get-tuple-element.8.refs_2_), custom_call_target="tpu_custom_call" | custom-call | tf_op jit(solution)/shard_map/pallas_call | solution.py:649
